TPU v7x, 128 devices: a whole 4x4x4 slice. The times are simulated.
128 devices in a mesh: dp: 8 (over y, z_lo), ctx: 4 (over z_hi, core), head: 4 (over x).
Axes of the slice: x: 4, y: 4, z: 4 (z_hi: 2, z_lo: 2; z = z_hi * 2 + z_lo), core: 2. Of those that a mesh axis runs over, the one named last changes fastest.
Arguments:
- inputs: bfloat16 [16, 1024, 1536], P('dp', ('ctx', 'head')), may hold values from -6 to 6
- positions: int32 [16, 1024], P('dp', ('ctx', 'head')), may hold values from 0 to 2047
- cotangent: bfloat16 [16, 1024, 1536], P('dp', ('ctx', 'head')), may hold values from -6 to 6
- attn_gain: bfloat16 [2, 1536], P(None, ('dp', 'ctx')), may hold values from 0.5 to 1.5
- query_weight: bfloat16 [2, 1536, 1536], P(None, ('dp', 'ctx')), may hold values from -0.15625 to 0.15625
- key_matrix: bfloat16 [2, 1536, 768], P(None, ('dp', 'ctx')), may hold values from -0.15625 to 0.15625
- value_matrix: bfloat16 [2, 1536, 768], P(None, ('dp', 'ctx')), may hold values from -0.15625 to 0.15625
- out_weight: bfloat16 [2, 1536, 1536], P(None, ('dp', 'ctx')), may hold values from -2.5 to 2.5
- mlp_gain: bfloat16 [2, 1536], P(None, ('dp', 'ctx')), may hold values from 0.5 to 1.5
- gate_weight: bfloat16 [2, 1536, 4096], P(None, ('dp', 'ctx')), may hold values from -0.15625 to 0.15625
- up_weight: bfloat16 [2, 1536, 4096], P(None, ('dp', 'ctx')), may hold values from -0.15625 to 0.15625
- down_weight: bfloat16 [2, 4096, 1536], P(None, ('dp', 'ctx')), may hold values from -0.09375 to 0.09375
Outputs:
- output: bfloat16 [16, 1024, 1536], P('dp', ('ctx', 'head'))
- input_grad: float32 [16, 1024, 1536], P('dp', ('ctx', 'head'))
- grad_attn_gain: float32 [2, 1536], P(None, ('dp', 'ctx'))
- grad_query_weight: float32 [2, 1536, 1536], P(None, ('dp', 'ctx'))
- grad_key_weight: float32 [2, 1536, 768], P(None, ('dp', 'ctx'))
- grad_value_weight: float32 [2, 1536, 768], P(None, ('dp', 'ctx'))
- grad_out_weight: float32 [2, 1536, 1536], P(None, ('dp', 'ctx'))
- grad_mlp_gain: float32 [2, 1536], P(None, ('dp', 'ctx'))
- grad_gate_weight: float32 [2, 1536, 4096], P(None, ('dp', 'ctx'))
- grad_up_weight: float32 [2, 1536, 4096], P(None, ('dp', 'ctx'))
- grad_down_weight: float32 [2, 4096, 1536], P(None, ('dp', 'ctx'))
All inputs are finite; a program needn't handle non-finite values.
Results may differ from a plain program's by a relative error of at most 0.035.
Values may be sent and summed in bfloat16 or wider, within the bound.
A program may use at most 320 MiB of HBM per device.

v0:
```python
from functools import partial

import jax
import jax.numpy as jnp
from jax import lax
from jax.sharding import PartitionSpec as P

HEAD_SIZE = 96
DECODER_LAYERS = 2


EPS = 1e-05
BASE = 100000.0
NEG = -1e30


def rope_tables(positions, head_width):
    half_width = head_width // 2
    frequency = BASE ** (-(jnp.arange(half_width, dtype=jnp.float32) * 2.0 / head_width))
    angles = positions.astype(jnp.float32)[..., None] * frequency
    return (jnp.cos(angles), jnp.sin(angles))


def rotate(tensor, cosine, sine_table):
    half_width = tensor.shape[-1] // 2
    first = tensor[..., :half_width]
    second = tensor[..., half_width:]
    cos_b = cosine[..., None, :]
    sin_b = sine_table[..., None, :]
    return jnp.concatenate(
        [first * cos_b - second * sin_b, second * cos_b + first * sin_b], axis=-1
    )


def norm_parts(hidden, gain):
    scale_row = lax.rsqrt(jnp.mean(hidden * hidden, axis=-1, keepdims=True) + EPS)
    return ((hidden * scale_row * gain.astype(jnp.float32)).astype(jnp.bfloat16), scale_row)


def norm_back(hidden, scale_row, gain, upstream):
    unit = hidden * scale_row
    gain_grad = jnp.sum(upstream * unit, axis=(0, 1))
    weighted = upstream * gain.astype(jnp.float32)
    return (
        scale_row * (weighted - unit * jnp.mean(weighted * unit, axis=-1, keepdims=True)),
        gain_grad,
    )


def per_block(making, blank, blocks, cycle_place, axis_out):
    pieces = [
        lax.cond(block_idx <= cycle_place, partial(making, block_idx), lambda: blank)
        for block_idx in range(blocks)
    ]
    return jnp.concatenate(pieces, axis=axis_out)


def score_blocks(queries, keys, cycle_place):
    row_count, kv_heads, reps, head_width = queries.shape
    blocks = keys.shape[0] // row_count
    scale = head_width ** (-0.5)
    query_pos = cycle_place * row_count + lax.broadcasted_iota(jnp.int32, (row_count, row_count), 0)

    def making(block_idx):
        key_block = keys[block_idx * row_count : (block_idx + 1) * row_count]
        raw = (
            jnp.einsum("qgrd,kgd->grqk", queries, key_block, preferred_element_type=jnp.float32)
            * scale
        )
        key_pos = block_idx * row_count + lax.broadcasted_iota(jnp.int32, (row_count, row_count), 1)
        return jnp.where(key_pos <= query_pos, raw, NEG)

    blank = jnp.full((kv_heads, reps, row_count, row_count), NEG, jnp.float32)
    return per_block(making, blank, blocks, cycle_place, 3)


def block_products(left, right, cycle_place, form):
    row_count = left.shape[2]
    blocks = right.shape[0] // row_count
    blank = jnp.zeros((row_count, left.shape[0], left.shape[1], right.shape[-1]), jnp.float32)
    result = blank
    for block_idx in range(blocks):
        left_block = left[..., block_idx * row_count : (block_idx + 1) * row_count]
        right_block = right[block_idx * row_count : (block_idx + 1) * row_count]

        def making(left_block=left_block, right_block=right_block):
            return jnp.einsum(form, left_block, right_block, preferred_element_type=jnp.float32)

        result = result + lax.cond(block_idx <= cycle_place, making, lambda: blank)
    return result


def attend_forward(queries, keys, values, cycle_place):
    scores = score_blocks(queries, keys, cycle_place)
    row_max = jnp.max(scores, axis=-1, keepdims=True)
    exponent = jnp.exp(scores - row_max)
    totals = jnp.sum(exponent, axis=-1, keepdims=True)
    probability = (exponent / totals).astype(jnp.bfloat16)
    mixed = block_products(probability, values, cycle_place, "grqk,kgd->qgrd")
    return (mixed, row_max + jnp.log(totals))


def attend_backward(queries, keys, values, log_total, grad_mixed, cycle_place):
    row_count, kv_heads, reps, head_width = queries.shape
    blocks = keys.shape[0] // row_count
    scale = head_width ** (-0.5)
    probability = jnp.exp(score_blocks(queries, keys, cycle_place) - log_total)
    rounded = probability.astype(jnp.bfloat16)

    def prob_block(block_idx):
        value_block = values[block_idx * row_count : (block_idx + 1) * row_count]
        return jnp.einsum(
            "qgrd,kgd->grqk", grad_mixed, value_block, preferred_element_type=jnp.float32
        )

    blank_scores = jnp.zeros((kv_heads, reps, row_count, row_count), jnp.float32)
    grad_prob = per_block(prob_block, blank_scores, blocks, cycle_place, 3)
    delta = jnp.sum(probability * grad_prob, axis=-1, keepdims=True)
    grad_score = (probability * (grad_prob - delta)).astype(jnp.bfloat16)
    grad_query = block_products(grad_score, keys, cycle_place, "grqk,kgd->qgrd") * scale

    def key_block_grad(block_idx):
        piece = grad_score[..., block_idx * row_count : (block_idx + 1) * row_count]
        return (
            jnp.einsum("grqk,qgrd->kgd", piece, queries, preferred_element_type=jnp.float32) * scale
        )

    def value_block_grad(block_idx):
        piece = rounded[..., block_idx * row_count : (block_idx + 1) * row_count]
        return jnp.einsum("grqk,qgrd->kgd", piece, grad_mixed, preferred_element_type=jnp.float32)

    blank_keys = jnp.zeros((row_count, kv_heads, head_width), jnp.float32)
    grad_key = per_block(key_block_grad, blank_keys, blocks, cycle_place, 0)
    grad_value = per_block(value_block_grad, blank_keys, blocks, cycle_place, 0)
    return (grad_query, grad_key, grad_value)


def gather_layer(shards, layer_idx):
    pieces = [member[layer_idx] for member in shards]
    return (
        lax.all_gather(pieces[0], ("dp", "ctx"), axis=0, tiled=True),
        lax.all_gather(pieces[1], ("dp", "ctx"), axis=0, tiled=True),
        lax.all_gather(pieces[2], ("dp", "ctx"), axis=0, tiled=True),
        lax.all_gather(pieces[3], ("dp", "ctx"), axis=0, tiled=True),
        lax.all_gather(pieces[4], ("dp", "ctx"), axis=0, tiled=True),
        lax.all_gather(pieces[5], ("dp", "ctx"), axis=0, tiled=True),
        lax.all_gather(pieces[6], ("dp", "ctx"), axis=0, tiled=True),
        lax.all_gather(pieces[7], ("dp", "ctx"), axis=0, tiled=True),
        lax.all_gather(pieces[8], ("dp", "ctx"), axis=0, tiled=True),
    )


def regather_layer(shards, layer_idx):
    pieces = [member[layer_idx] for member in shards]
    return (
        lax.all_gather(pieces[0], ("dp", "ctx"), axis=0, tiled=True),
        lax.all_gather(pieces[1], ("dp", "ctx"), axis=0, tiled=True),
        lax.all_gather(pieces[2], ("dp", "ctx"), axis=0, tiled=True),
        lax.all_gather(pieces[3], ("dp", "ctx"), axis=0, tiled=True),
        lax.all_gather(pieces[4], ("dp", "ctx"), axis=0, tiled=True),
        lax.all_gather(pieces[5], ("dp", "ctx"), axis=0, tiled=True),
        lax.all_gather(pieces[6], ("dp", "ctx"), axis=0, tiled=True),
        lax.all_gather(pieces[7], ("dp", "ctx"), axis=0, tiled=True),
        lax.all_gather(pieces[8], ("dp", "ctx"), axis=0, tiled=True),
    )


def layer_forward(hidden, weight_set, cosine, sine_table, cycle_place):
    (
        attn_gain,
        query_weight,
        key_matrix,
        value_matrix,
        out_weight,
        mlp_gain,
        gate_weight,
        up_weight,
        down_weight,
    ) = weight_set
    seqs_dev, tok_dev = (hidden.shape[0], hidden.shape[1])
    normalized_rows, scale_one = norm_parts(hidden, attn_gain)
    query_p = jnp.einsum(
        "std,de->ste", normalized_rows, query_weight, preferred_element_type=jnp.float32
    )
    key_projected = jnp.einsum(
        "std,de->ste", normalized_rows, key_matrix, preferred_element_type=jnp.float32
    )
    value_broadcast = jnp.einsum(
        "std,de->ste", normalized_rows, value_matrix, preferred_element_type=jnp.float32
    ).astype(jnp.bfloat16)
    query_r = (
        rotate(query_p.reshape(seqs_dev, tok_dev, -1, HEAD_SIZE), cosine, sine_table)
        .reshape(seqs_dev, tok_dev, -1)
        .astype(jnp.bfloat16)
    )
    key_r = (
        rotate(key_projected.reshape(seqs_dev, tok_dev, -1, HEAD_SIZE), cosine, sine_table)
        .reshape(seqs_dev, tok_dev, -1)
        .astype(jnp.bfloat16)
    )
    query_h, key_h, value_h = (
        lax.all_to_all(query_r, "head", split_axis=2, concat_axis=1, tiled=True),
        lax.all_to_all(key_r, "head", split_axis=2, concat_axis=1, tiled=True),
        lax.all_to_all(value_broadcast, "head", split_axis=2, concat_axis=1, tiled=True),
    )
    key_all, value_all = (
        lax.all_gather(key_h, "ctx", axis=1, tiled=True),
        lax.all_gather(value_h, "ctx", axis=1, tiled=True),
    )
    kv_heads = key_h.shape[2] // HEAD_SIZE
    reps = query_h.shape[2] // HEAD_SIZE // kv_heads
    row_count = query_h.shape[1]
    queries = query_h.reshape(seqs_dev, row_count, kv_heads, reps, HEAD_SIZE)
    keys = key_all.reshape(seqs_dev, -1, kv_heads, HEAD_SIZE)
    values = value_all.reshape(seqs_dev, -1, kv_heads, HEAD_SIZE)
    mixed, log_total = lax.map(
        lambda operand: attend_forward(operand[0], operand[1], operand[2], cycle_place),
        (queries, keys, values),
    )
    mixed_b = mixed.reshape(seqs_dev, row_count, -1).astype(jnp.bfloat16)
    mixed_tok = lax.all_to_all(mixed_b, "head", split_axis=1, concat_axis=2, tiled=True)
    residual = hidden + jnp.einsum(
        "ste,ed->std", mixed_tok, out_weight, preferred_element_type=jnp.float32
    )
    normed_two, scale_two = norm_parts(residual, mlp_gain)
    gate = jnp.einsum("std,df->stf", normed_two, gate_weight, preferred_element_type=jnp.float32)
    up_proj = jnp.einsum("std,df->stf", normed_two, up_weight, preferred_element_type=jnp.float32)
    activ = (jax.nn.silu(gate) * up_proj).astype(jnp.bfloat16)
    result = residual + jnp.einsum(
        "stf,fd->std", activ, down_weight, preferred_element_type=jnp.float32
    )
    cache = (
        hidden,
        normalized_rows,
        scale_one,
        queries,
        keys,
        values,
        log_total,
        mixed_tok,
        residual,
        normed_two,
        scale_two,
        gate,
        up_proj,
        activ,
    )
    return (result, cache)


def layer_backward(gradient, weight_set, cache, cosine, sine_table, cycle_place):
    (
        attn_gain,
        query_weight,
        key_matrix,
        value_matrix,
        out_weight,
        mlp_gain,
        gate_weight,
        up_weight,
        down_weight,
    ) = weight_set
    (
        hidden,
        normalized_rows,
        scale_one,
        queries,
        keys,
        values,
        log_total,
        mixed_tok,
        residual,
        normed_two,
        scale_two,
        gate,
        up_proj,
        activ,
    ) = cache
    grad_b = gradient.astype(jnp.bfloat16)
    grad_down = jnp.einsum("stf,std->fd", activ, grad_b, preferred_element_type=jnp.float32)
    grad_act = jnp.einsum("std,fd->stf", grad_b, down_weight, preferred_element_type=jnp.float32)
    sigma = jax.nn.sigmoid(gate)
    grad_gate = (grad_act * up_proj * sigma * (1.0 + gate * (1.0 - sigma))).astype(jnp.bfloat16)
    grad_up = (grad_act * gate * sigma).astype(jnp.bfloat16)
    grad_gate_w = jnp.einsum(
        "std,stf->df", normed_two, grad_gate, preferred_element_type=jnp.float32
    )
    grad_up_w = jnp.einsum("std,stf->df", normed_two, grad_up, preferred_element_type=jnp.float32)
    grad_normed = jnp.einsum(
        "stf,df->std", grad_gate, gate_weight, preferred_element_type=jnp.float32
    )
    grad_normed = grad_normed + jnp.einsum(
        "stf,df->std", grad_up, up_weight, preferred_element_type=jnp.float32
    )
    grad_norm_two, grad_mlp_gain = norm_back(residual, scale_two, mlp_gain, grad_normed)
    grad_res = gradient + grad_norm_two
    grad_rb = grad_res.astype(jnp.bfloat16)
    grad_out_w = jnp.einsum("ste,std->ed", mixed_tok, grad_rb, preferred_element_type=jnp.float32)
    grad_mix = jnp.einsum(
        "std,ed->ste", grad_rb, out_weight, preferred_element_type=jnp.float32
    ).astype(jnp.bfloat16)
    grad_mix_h = lax.all_to_all(grad_mix, "head", split_axis=2, concat_axis=1, tiled=True)
    seqs_dev, row_count = (grad_mix_h.shape[0], grad_mix_h.shape[1])
    grad_mix_h = grad_mix_h.reshape(queries.shape)
    grad_query, grad_key, grad_value = lax.map(
        lambda operand: attend_backward(
            operand[0], operand[1], operand[2], operand[3], operand[4], cycle_place
        ),
        (queries, keys, values, log_total, grad_mix_h),
    )
    kv_cols = keys.shape[2] * keys.shape[3]
    key_sum, value_sum = (
        lax.psum_scatter(
            grad_key.reshape(seqs_dev, -1, kv_cols).astype(jnp.bfloat16),
            "ctx",
            scatter_dimension=1,
            tiled=True,
        ).astype(jnp.float32),
        lax.psum_scatter(
            grad_value.reshape(seqs_dev, -1, kv_cols).astype(jnp.bfloat16),
            "ctx",
            scatter_dimension=1,
            tiled=True,
        ).astype(jnp.float32),
    )
    grad_q_b = grad_query.reshape(seqs_dev, row_count, -1).astype(jnp.bfloat16)
    back_q, back_k, back_v = (
        lax.all_to_all(grad_q_b, "head", split_axis=1, concat_axis=2, tiled=True),
        lax.all_to_all(
            key_sum.astype(jnp.bfloat16), "head", split_axis=1, concat_axis=2, tiled=True
        ),
        lax.all_to_all(
            value_sum.astype(jnp.bfloat16), "head", split_axis=1, concat_axis=2, tiled=True
        ),
    )
    tok_dev = back_q.shape[1]
    grad_qp = (
        rotate(
            back_q.astype(jnp.float32).reshape(seqs_dev, tok_dev, -1, HEAD_SIZE),
            cosine,
            -sine_table,
        )
        .reshape(seqs_dev, tok_dev, -1)
        .astype(jnp.bfloat16)
    )
    grad_kp = (
        rotate(
            back_k.astype(jnp.float32).reshape(seqs_dev, tok_dev, -1, HEAD_SIZE),
            cosine,
            -sine_table,
        )
        .reshape(seqs_dev, tok_dev, -1)
        .astype(jnp.bfloat16)
    )
    grad_query_w = jnp.einsum(
        "std,ste->de", normalized_rows, grad_qp, preferred_element_type=jnp.float32
    )
    grad_key_w = jnp.einsum(
        "std,ste->de", normalized_rows, grad_kp, preferred_element_type=jnp.float32
    )
    grad_value_w = jnp.einsum(
        "std,ste->de", normalized_rows, back_v, preferred_element_type=jnp.float32
    )
    grad_normed_one = jnp.einsum(
        "ste,de->std", grad_qp, query_weight, preferred_element_type=jnp.float32
    )
    grad_normed_one = grad_normed_one + jnp.einsum(
        "ste,de->std", grad_kp, key_matrix, preferred_element_type=jnp.float32
    )
    grad_normed_one = grad_normed_one + jnp.einsum(
        "ste,de->std", back_v, value_matrix, preferred_element_type=jnp.float32
    )
    grad_norm_one, grad_attn_gain = norm_back(hidden, scale_one, attn_gain, grad_normed_one)
    grads = (
        grad_attn_gain,
        grad_query_w,
        grad_key_w,
        grad_value_w,
        grad_out_w,
        grad_mlp_gain,
        grad_gate_w,
        grad_up_w,
        grad_down,
    )
    return (grad_res + grad_norm_one, grads)


def reduce_grads(grads):
    shard_sums = (
        lax.psum_scatter(
            grads[0].astype(jnp.bfloat16), ("dp", "ctx"), scatter_dimension=0, tiled=True
        ).astype(jnp.float32),
        lax.psum_scatter(
            grads[1].astype(jnp.bfloat16), ("dp", "ctx"), scatter_dimension=0, tiled=True
        ).astype(jnp.float32),
        lax.psum_scatter(
            grads[2].astype(jnp.bfloat16), ("dp", "ctx"), scatter_dimension=0, tiled=True
        ).astype(jnp.float32),
        lax.psum_scatter(
            grads[3].astype(jnp.bfloat16), ("dp", "ctx"), scatter_dimension=0, tiled=True
        ).astype(jnp.float32),
        lax.psum_scatter(
            grads[4].astype(jnp.bfloat16), ("dp", "ctx"), scatter_dimension=0, tiled=True
        ).astype(jnp.float32),
        lax.psum_scatter(
            grads[5].astype(jnp.bfloat16), ("dp", "ctx"), scatter_dimension=0, tiled=True
        ).astype(jnp.float32),
        lax.psum_scatter(
            grads[6].astype(jnp.bfloat16), ("dp", "ctx"), scatter_dimension=0, tiled=True
        ).astype(jnp.float32),
        lax.psum_scatter(
            grads[7].astype(jnp.bfloat16), ("dp", "ctx"), scatter_dimension=0, tiled=True
        ).astype(jnp.float32),
        lax.psum_scatter(
            grads[8].astype(jnp.bfloat16), ("dp", "ctx"), scatter_dimension=0, tiled=True
        ).astype(jnp.float32),
    )
    return (
        lax.psum(shard_sums[0].astype(jnp.bfloat16), "head").astype(jnp.float32),
        lax.psum(shard_sums[1].astype(jnp.bfloat16), "head").astype(jnp.float32),
        lax.psum(shard_sums[2].astype(jnp.bfloat16), "head").astype(jnp.float32),
        lax.psum(shard_sums[3].astype(jnp.bfloat16), "head").astype(jnp.float32),
        lax.psum(shard_sums[4].astype(jnp.bfloat16), "head").astype(jnp.float32),
        lax.psum(shard_sums[5].astype(jnp.bfloat16), "head").astype(jnp.float32),
        lax.psum(shard_sums[6].astype(jnp.bfloat16), "head").astype(jnp.float32),
        lax.psum(shard_sums[7].astype(jnp.bfloat16), "head").astype(jnp.float32),
        lax.psum(shard_sums[8].astype(jnp.bfloat16), "head").astype(jnp.float32),
    )


def per_device(
    inputs,
    positions,
    cotangent,
    attn_gain,
    query_weight,
    key_matrix,
    value_matrix,
    out_weight,
    mlp_gain,
    gate_weight,
    up_weight,
    down_weight,
):
    shards = (
        attn_gain,
        query_weight,
        key_matrix,
        value_matrix,
        out_weight,
        mlp_gain,
        gate_weight,
        up_weight,
        down_weight,
    )
    cycle_place = lax.axis_index("ctx")
    cosine, sine_table = rope_tables(positions, HEAD_SIZE)
    hidden = inputs.astype(jnp.float32)
    caches = []
    gathered = []
    for layer_idx in range(DECODER_LAYERS):
        weight_set = gather_layer(shards, layer_idx)
        gathered.append(weight_set)
        hidden, cache = layer_forward(hidden, weight_set, cosine, sine_table, cycle_place)
        caches.append(cache)
    output = hidden.astype(jnp.bfloat16)
    gradient = cotangent.astype(jnp.float32)
    reduced = [None] * DECODER_LAYERS
    for layer_idx in reversed(range(DECODER_LAYERS)):
        weight_set = regather_layer(shards, layer_idx)
        gradient, grads = layer_backward(
            gradient, weight_set, caches[layer_idx], cosine, sine_table, cycle_place
        )
        reduced[layer_idx] = reduce_grads(grads)
    stacked = [
        jnp.stack([reduced[layer_idx][member] for layer_idx in range(DECODER_LAYERS)])
        for member in range(9)
    ]
    return (
        output,
        gradient,
        stacked[0],
        stacked[1],
        stacked[2],
        stacked[3],
        stacked[4],
        stacked[5],
        stacked[6],
        stacked[7],
        stacked[8],
    )


def solution(mesh):
    placed = (
        P("dp", ("ctx", "head"), None),
        P("dp", ("ctx", "head")),
        P("dp", ("ctx", "head"), None),
        P(None, ("dp", "ctx")),
        P(None, ("dp", "ctx"), None),
        P(None, ("dp", "ctx"), None),
        P(None, ("dp", "ctx"), None),
        P(None, ("dp", "ctx"), None),
        P(None, ("dp", "ctx")),
        P(None, ("dp", "ctx"), None),
        P(None, ("dp", "ctx"), None),
        P(None, ("dp", "ctx"), None),
    )
    return jax.shard_map(
        per_device,
        mesh=mesh,
        in_specs=placed,
        out_specs=(
            P("dp", ("ctx", "head"), None),
            P("dp", ("ctx", "head"), None),
            P(None, ("dp", "ctx")),
            P(None, ("dp", "ctx"), None),
            P(None, ("dp", "ctx"), None),
            P(None, ("dp", "ctx"), None),
            P(None, ("dp", "ctx"), None),
            P(None, ("dp", "ctx")),
            P(None, ("dp", "ctx"), None),
            P(None, ("dp", "ctx"), None),
            P(None, ("dp", "ctx"), None),
        ),
        check_vma=False,
    )
```

profile of v0, /device:TPU:0, one launch (start us, length us, event | category | flops | bytes accessed | tf_op | source)
XLA Modules:
  0.0 3721.3 jit_solution(11860811243781182894)
XLA Ops:
  25.5 129.9 %all-reduce.9 = (bf16[1536]{0:T(1024)(128)(2,1)S(1)}, bf16[1536]{0:T(1024)(128)(2,1)}, bf16[1536]{0:T(1024)(128)(2,1)}, bf16[1536]{0:T(1024)(128)(2,1)S(1)}) all-reduce(bf16[1536]{0:T(1024)(128)(2,1)S(1)} %dynamic-update-slice, bf16[1536]{0:T(1024)(128)(2,1)S(1)} %dynamic-update-slice.1, ...), channel_id=2, replica_groups=mesh['dp'=8,'ctx'=4,'head'=4] {'dp','ctx'}, use_global_device_ids=true, to_apply=%add | all-reduce | flops 6144 | bytes 24576
  228.9 41.7 %while.60 = (s32[]{:T(128)}, bf16[2,256,2,2,96]{1,4,3,2,0:T(8,128)(2,1)}, f32[2,2,2,256,1]{3,2,1,4,0:T(2,128)}, pred[]{:T(512)}, bf16[2,1024,2,96]{1,3,2,0:T(8,1...) while((s32[]{:T(128)}, ...), condition=%wide.region_23.24_spmd, body=%wide.region_1.23_spmd.sunk | while | flops 417890304 | bytes 69345984 | solution.py:216
  289.2 52.1 %all-gather.41.cloned.1.call-done = bf16[1,1536,4096]{2,1,0:T(8,128)(2,1)} async-done(((bf16[1,48,4096]{2,1,0:T(8,128)(2,1)}), bf16[1,1536,4096]{2,1,0:T(8,128)(2,1)}) %all-gather.41.cloned.1.call-update) | async-done | bytes 12582928 | tf_op jit(solution)/shard_map/all_gather | solution.py:147
  349.0 70.9 %all-gather.43.cloned.1.call-done = bf16[1,1536,4096]{2,1,0:T(8,128)(2,1)} async-done(((bf16[1,48,4096]{2,1,0:T(8,128)(2,1)}), bf16[1,1536,4096]{2,1,0:T(8,128)(2,1)}) %all-gather.43.cloned.1.call-update) | async-done | bytes 12582928 | tf_op jit(solution)/shard_map/all_gather | solution.py:148
  428.5 70.0 %all-gather.45.cloned.1.call-done = bf16[1,4096,1536]{2,1,0:T(8,128)(2,1)} async-done(((bf16[1,128,1536]{2,1,0:T(8,128)(2,1)}), bf16[1,4096,1536]{2,1,0:T(8,128)(2,1)}) %all-gather.45.cloned.1.call-update) | async-done | bytes 12582928 | tf_op jit(solution)/shard_map/all_gather | solution.py:149
  506.1 55.8 %all-gather.51.cloned.1.call-done = bf16[1,1536,1536]{2,1,0:T(8,128)(2,1)} async-done(((bf16[1,48,1536]{2,1,0:T(8,128)(2,1)}), bf16[1,1536,1536]{2,1,0:T(8,128)(2,1)}) %all-gather.51.cloned.1.call-update) | async-done | bytes 4718608 | tf_op jit(solution)/shard_map/all_gather | solution.py:142
  565.4 55.6 %all-gather.49.cloned.1.call-done = bf16[1,1536,768]{2,1,0:T(8,128)(2,1)} async-done(((bf16[1,48,768]{2,1,0:T(8,128)(2,1)}), bf16[1,1536,768]{2,1,0:T(8,128)(2,1)}) %all-gather.49.cloned.1.call-update) | async-done | bytes 2359312 | tf_op jit(solution)/shard_map/all_gather | solution.py:143
  629.4 50.4 %all-gather.47.cloned.1.call-done = bf16[1,1536,768]{2,1,0:T(8,128)(2,1)} async-done(((bf16[1,48,768]{2,1,0:T(8,128)(2,1)}), bf16[1,1536,768]{2,1,0:T(8,128)(2,1)}) %all-gather.47.cloned.1.call-update) | async-done | bytes 2359312 | tf_op jit(solution)/shard_map/all_gather | solution.py:144
  737.3 43.4 %while.61 = (s32[]{:T(128)}, bf16[2,256,2,2,96]{1,4,3,2,0:T(8,128)(2,1)}, f32[2,2,2,256,1]{3,2,1,4,0:T(2,128)S(1)}, pred[]{:T(512)}, bf16[2,1024,2,96]{1,3,2,0:T...) while((s32[]{:T(128)}, ...), condition=%wide.region_48.49_spmd, body=%wide.region_26.48_spmd.sunk | while | flops 417890304 | bytes 62988880 | solution.py:216
  798.0 33.3 all-gather.53.cloned.1.call-done
  834.8 74.2 %all-gather.57.cloned.1.call-done = bf16[1,1536,4096]{2,1,0:T(8,128)(2,1)} async-done(((bf16[1,48,4096]{2,1,0:T(8,128)(2,1)}), bf16[1,1536,4096]{2,1,0:T(8,128)(2,1)}) %all-gather.57.cloned.1.call-update) | async-done | bytes 12582928 | tf_op jit(solution)/shard_map/all_gather | solution.py:148
  916.7 70.8 %all-gather.55.cloned.1.call-done = bf16[1,1536,4096]{2,1,0:T(8,128)(2,1)} async-done(((bf16[1,48,4096]{2,1,0:T(8,128)(2,1)}), bf16[1,1536,4096]{2,1,0:T(8,128)(2,1)}) %all-gather.55.cloned.1.call-update) | async-done | bytes 12582928 | tf_op jit(solution)/shard_map/all_gather | solution.py:147
  1035.3 80.8 %while.62 = (s32[]{:T(128)}, bf16[2,256,2,2,96]{1,4,3,2,0:T(8,128)(2,1)}, bf16[2,1024,2,96]{1,3,2,0:T(8,128)(2,1)}, bf16[2,1024,2,96]{1,3,2,0:T(8,128)(2,1)}, pr...) while((s32[]{:T(128)}, ...), condition=%wide.region_93.94_spmd, body=%wide.region_51.93_spmd.sunk | while | flops 1030753280 | bytes 85747320 | solution.py:305
  1130.4 51.0 %reduce-scatter.19.cloned.1.call-done = bf16[2,256,192]{1,2,0:T(8,128)(2,1)} async-done(((bf16[2,1024,192]{1,2,0:T(8,128)(2,1)}), bf16[2,256,192]{1,2,0:T(8,128)(2,1)}) %reduce-scatter.19.cloned.1.call-update) | async-done | bytes 196624 | tf_op jit(solution)/shard_map/reduce_scatter | solution.py:313
  1192.3 21.3 reduce-scatter.21.cloned.1.call-done
  1287.0 88.0 %while.63 = (s32[]{:T(128)}, bf16[2,256,2,2,96]{1,4,3,2,0:T(8,128)(2,1)}, bf16[2,1024,2,96]{1,3,2,0:T(8,128)(2,1)}, bf16[2,1024,2,96]{1,3,2,0:T(8,128)(2,1)}, pr...) while((s32[]{:T(128)}, ...), condition=%wide.region_140.141_spmd, body=%wide.region_98.140_spmd.sunk | while | flops 1030753280 | bytes 81028664 | solution.py:305
  1381.5 59.8 %reduce-scatter.23.cloned.1.call-done = bf16[2,256,192]{1,2,0:T(8,128)(2,1)} async-done(((bf16[2,1024,192]{1,2,0:T(8,128)(2,1)}), bf16[2,256,192]{1,2,0:T(8,128)(2,1)}) %reduce-scatter.23.cloned.1.call-update) | async-done | bytes 196624 | tf_op jit(solution)/shard_map/reduce_scatter | solution.py:313
  1566.3 44.9 %reduce-scatter.33.cloned.1.call-done = bf16[48,768]{1,0:T(8,128)(2,1)} async-done(((bf16[1536,768]{1,0:T(8,128)(2,1)}), bf16[48,768]{1,0:T(8,128)(2,1)}) %reduce-scatter.33.cloned.1.call-update) | async-done | bytes 73744 | tf_op jit(solution)/shard_map/reduce_scatter | solution.py:396
  1611.2 134.8 %reduce-scatter.37.cloned.1.call-done = bf16[48,768]{1,0:T(8,128)(2,1)} async-done(((bf16[1536,768]{1,0:T(8,128)(2,1)}), bf16[48,768]{1,0:T(8,128)(2,1)}) %reduce-scatter.37.cloned.1.call-update) | async-done | bytes 73744 | tf_op jit(solution)/shard_map/reduce_scatter | solution.py:399
  1746.0 134.7 %reduce-scatter.31.cloned.1.call-done = bf16[48,768]{1,0:T(8,128)(2,1)} async-done(((bf16[1536,768]{1,0:T(8,128)(2,1)}), bf16[48,768]{1,0:T(8,128)(2,1)}) %reduce-scatter.31.cloned.1.call-update) | async-done | bytes 73744 | tf_op jit(solution)/shard_map/reduce_scatter | solution.py:396
  1880.7 134.7 %reduce-scatter.35.cloned.1.call-done = bf16[48,768]{1,0:T(8,128)(2,1)} async-done(((bf16[1536,768]{1,0:T(8,128)(2,1)}), bf16[48,768]{1,0:T(8,128)(2,1)}) %reduce-scatter.35.cloned.1.call-update) | async-done | bytes 73744 | tf_op jit(solution)/shard_map/reduce_scatter | solution.py:399
  2015.4 141.1 %reduce-scatter.41.cloned.1.call-done = bf16[48,1536]{1,0:T(8,128)(2,1)} async-done(((bf16[1536,1536]{1,0:T(8,128)(2,1)}), bf16[48,1536]{1,0:T(8,128)(2,1)}) %reduce-scatter.41.cloned.1.call-update) | async-done | bytes 147472 | tf_op jit(solution)/shard_map/reduce_scatter | solution.py:402
  2156.5 141.6 %reduce-scatter.29.cloned.1.call-done = bf16[48,1536]{1,0:T(8,128)(2,1)} async-done(((bf16[1536,1536]{1,0:T(8,128)(2,1)}), bf16[48,1536]{1,0:T(8,128)(2,1)}) %reduce-scatter.29.cloned.1.call-update) | async-done | bytes 147472 | tf_op jit(solution)/shard_map/reduce_scatter | solution.py:393
  2298.1 141.3 %reduce-scatter.39.cloned.1.call-done = bf16[48,1536]{1,0:T(8,128)(2,1)} async-done(((bf16[1536,1536]{1,0:T(8,128)(2,1)}), bf16[48,1536]{1,0:T(8,128)(2,1)}) %reduce-scatter.39.cloned.1.call-update) | async-done | bytes 147472 | tf_op jit(solution)/shard_map/reduce_scatter | solution.py:402
  2439.3 141.4 %reduce-scatter.27.cloned.1.call-done = bf16[48,1536]{1,0:T(8,128)(2,1)} async-done(((bf16[1536,1536]{1,0:T(8,128)(2,1)}), bf16[48,1536]{1,0:T(8,128)(2,1)}) %reduce-scatter.27.cloned.1.call-update) | async-done | bytes 147472 | tf_op jit(solution)/shard_map/reduce_scatter | solution.py:393
  2580.7 160.4 %reduce-scatter.45.cloned.1.call-done = bf16[48,4096]{1,0:T(8,128)(2,1)} async-done(((bf16[1536,4096]{1,0:T(8,128)(2,1)}), bf16[48,4096]{1,0:T(8,128)(2,1)}) %reduce-scatter.45.cloned.1.call-update) | async-done | bytes 393232 | tf_op jit(solution)/shard_map/reduce_scatter | solution.py:408
  2741.1 162.7 %reduce-scatter.49.cloned.1.call-done = bf16[48,4096]{1,0:T(8,128)(2,1)} async-done(((bf16[1536,4096]{1,0:T(8,128)(2,1)}), bf16[48,4096]{1,0:T(8,128)(2,1)}) %reduce-scatter.49.cloned.1.call-update) | async-done | bytes 393232 | tf_op jit(solution)/shard_map/reduce_scatter | solution.py:411
  2903.8 162.3 %reduce-scatter.53.cloned.1.call-done = bf16[128,1536]{1,0:T(8,128)(2,1)} async-done(((bf16[4096,1536]{1,0:T(8,128)(2,1)}), bf16[128,1536]{1,0:T(8,128)(2,1)}) %reduce-scatter.53.cloned.1.call-update) | async-done | bytes 393232 | tf_op jit(solution)/shard_map/reduce_scatter | solution.py:414
  3066.1 162.2 %reduce-scatter.51.cloned.1.call-done = bf16[128,1536]{1,0:T(8,128)(2,1)} async-done(((bf16[4096,1536]{1,0:T(8,128)(2,1)}), bf16[128,1536]{1,0:T(8,128)(2,1)}) %reduce-scatter.51.cloned.1.call-update) | async-done | bytes 393232 | tf_op jit(solution)/shard_map/reduce_scatter | solution.py:414
  3228.4 162.8 %reduce-scatter.43.cloned.1.call-done = bf16[48,4096]{1,0:T(8,128)(2,1)} async-done(((bf16[1536,4096]{1,0:T(8,128)(2,1)}), bf16[48,4096]{1,0:T(8,128)(2,1)}) %reduce-scatter.43.cloned.1.call-update) | async-done | bytes 393232 | tf_op jit(solution)/shard_map/reduce_scatter | solution.py:408
  3391.1 162.6 %reduce-scatter.47.cloned.1.call-done = bf16[48,4096]{1,0:T(8,128)(2,1)} async-done(((bf16[1536,4096]{1,0:T(8,128)(2,1)}), bf16[48,4096]{1,0:T(8,128)(2,1)}) %reduce-scatter.47.cloned.1.call-update) | async-done | bytes 393232 | tf_op jit(solution)/shard_map/reduce_scatter | solution.py:411
  3567.1 127.0 %all-reduce.8 = (bf16[1536]{0:T(1024)(128)(2,1)S(1)}, bf16[1536]{0:T(1024)(128)(2,1)S(1)}, bf16[1536]{0:T(1024)(128)(2,1)S(1)}, bf16[1536]{0:T(1024)(128)(2,1)S(1)}) all-reduce(bf16[1536]{0:T(1024)(128)(2,1)S(1)} %copy-done.112, ...), channel_id=25, replica_groups=mesh['dp'=8,'ctx'=4,'head'=4] {'dp','ctx'}, use_global_device_ids=true, to_apply=%region_148.149.clone | all-reduce | flops 6144 | bytes 24576
  (1002 shorter events, 863.0 us)
Async XLA Ops:
  7.2 149.4 %all-gather.35.cloned.1.call-start = ((), (), s32[]{:S(2)}) async-start(), calls=%async_computation.53 | async-start | bytes 2433024 | tf_op jit(solution)/shard_map/all_gather | solution.py:143
  9.0 156.1 %all-gather.33.cloned.1.call-start = ((), (), s32[]{:S(2)}) async-start(), calls=%async_computation.52 | async-start | bytes 2433024 | tf_op jit(solution)/shard_map/all_gather | solution.py:144
  10.6 186.7 %all-gather.37.cloned.1.call-start = ((), (), s32[]{:S(2)}) async-start(), calls=%async_computation.54 | async-start | bytes 4866048 | tf_op jit(solution)/shard_map/all_gather | solution.py:142
  12.5 273.1 %all-gather.39.cloned.1.call-start = ((), (), s32[]{:S(2)}) async-start(), calls=%async_computation.55 | async-start | bytes 4866048 | tf_op jit(solution)/shard_map/all_gather | solution.py:145
  14.3 327.0 %all-gather.41.cloned.1.call-start = ((), (), s32[]{:S(2)}) async-start(), calls=%async_computation.56 | async-start | bytes 12976128 | tf_op jit(solution)/shard_map/all_gather | solution.py:147
  16.4 403.4 %all-gather.43.cloned.1.call-start = ((), (), s32[]{:S(2)}) async-start(), calls=%async_computation.57 | async-start | bytes 12976128 | tf_op jit(solution)/shard_map/all_gather | solution.py:148
  17.5 481.1 %all-gather.45.cloned.1.call-start = ((), (), s32[]{:S(2)}) async-start(), calls=%async_computation.58 | async-start | bytes 12976128 | tf_op jit(solution)/shard_map/all_gather | solution.py:149
  18.5 543.4 %all-gather.51.cloned.1.call-start = ((), (), s32[]{:S(2)}) async-start(), calls=%async_computation.61 | async-start | bytes 4866048 | tf_op jit(solution)/shard_map/all_gather | solution.py:142
  19.2 601.7 %all-gather.49.cloned.1.call-start = ((), (), s32[]{:S(2)}) async-start(), calls=%async_computation.60 | async-start | bytes 2433024 | tf_op jit(solution)/shard_map/all_gather | solution.py:143
  20.0 659.7 %all-gather.47.cloned.1.call-start = ((), (), s32[]{:S(2)}) async-start(), calls=%async_computation.59 | async-start | bytes 2433024 | tf_op jit(solution)/shard_map/all_gather | solution.py:144
  20.6 767.1 %all-gather.59.cloned.1.call-start = ((), (), s32[]{:S(2)}) async-start(), calls=%async_computation.65 | async-start | bytes 12976128 | tf_op jit(solution)/shard_map/all_gather | solution.py:149
  21.3 810.1 %all-gather.53.cloned.1.call-start = ((), (), s32[]{:S(2)}) async-start(), calls=%async_computation.62 | async-start | bytes 4866048 | tf_op jit(solution)/shard_map/all_gather | solution.py:145
  21.9 887.1 %all-gather.57.cloned.1.call-start = ((), (), s32[]{:S(2)}) async-start(), calls=%async_computation.64 | async-start | bytes 12976128 | tf_op jit(solution)/shard_map/all_gather | solution.py:148
  22.6 964.9 %all-gather.55.cloned.1.call-start = ((), (), s32[]{:S(2)}) async-start(), calls=%async_computation.63 | async-start | bytes 12976128 | tf_op jit(solution)/shard_map/all_gather | solution.py:147
  1021.5 159.9 %reduce-scatter.19.cloned.1.call-start = ((), (), s32[]{:S(2)}) async-start(), calls=%async_computation.34 | async-start | bytes 983040 | tf_op jit(solution)/shard_map/reduce_scatter | solution.py:313
  1219.8 221.4 %reduce-scatter.23.cloned.1.call-start = ((), (), s32[]{:S(2)}) async-start(), calls=%async_computation.36 | async-start | bytes 983040 | tf_op jit(solution)/shard_map/reduce_scatter | solution.py:313
  1375.0 98.4 %reduce-scatter.25.cloned.1.call-start = ((), (), s32[]{:S(2)}) async-start(), calls=%async_computation.37 | async-start | bytes 983040 | tf_op jit(solution)/shard_map/reduce_scatter | solution.py:319
  1375.6 235.6 %reduce-scatter.33.cloned.1.call-start = ((), (), s32[]{:S(2)}) async-start(), calls=%async_computation.41 | async-start | bytes 2433024 | tf_op jit(solution)/shard_map/reduce_scatter | solution.py:396
  1379.1 366.9 %reduce-scatter.37.cloned.1.call-start = ((), (), s32[]{:S(2)}) async-start(), calls=%async_computation.43 | async-start | bytes 2433024 | tf_op jit(solution)/shard_map/reduce_scatter | solution.py:399
  1381.4 499.2 %reduce-scatter.31.cloned.1.call-start = ((), (), s32[]{:S(2)}) async-start(), calls=%async_computation.40 | async-start | bytes 2433024 | tf_op jit(solution)/shard_map/reduce_scatter | solution.py:396
  1456.9 558.5 %reduce-scatter.35.cloned.1.call-start = ((), (), s32[]{:S(2)}) async-start(), calls=%async_computation.42 | async-start | bytes 2433024 | tf_op jit(solution)/shard_map/reduce_scatter | solution.py:399
  1488.1 668.3 %reduce-scatter.41.cloned.1.call-start = ((), (), s32[]{:S(2)}) async-start(), calls=%async_computation.45 | async-start | bytes 4866048 | tf_op jit(solution)/shard_map/reduce_scatter | solution.py:402
  1491.8 806.3 %reduce-scatter.29.cloned.1.call-start = ((), (), s32[]{:S(2)}) async-start(), calls=%async_computation.39 | async-start | bytes 4866048 | tf_op jit(solution)/shard_map/reduce_scatter | solution.py:393
  1496.3 943.0 %reduce-scatter.39.cloned.1.call-start = ((), (), s32[]{:S(2)}) async-start(), calls=%async_computation.44 | async-start | bytes 4866048 | tf_op jit(solution)/shard_map/reduce_scatter | solution.py:402
  1501.2 1079.5 %reduce-scatter.27.cloned.1.call-start = ((), (), s32[]{:S(2)}) async-start(), calls=%async_computation.38 | async-start | bytes 4866048 | tf_op jit(solution)/shard_map/reduce_scatter | solution.py:393
  1518.8 1222.3 %reduce-scatter.45.cloned.1.call-start = ((), (), s32[]{:S(2)}) async-start(), calls=%async_computation.47 | async-start | bytes 12976128 | tf_op jit(solution)/shard_map/reduce_scatter | solution.py:408
  1526.6 1377.2 %reduce-scatter.49.cloned.1.call-start = ((), (), s32[]{:S(2)}) async-start(), calls=%async_computation.49 | async-start | bytes 12976128 | tf_op jit(solution)/shard_map/reduce_scatter | solution.py:411
  1534.3 1531.8 %reduce-scatter.53.cloned.1.call-start = ((), (), s32[]{:S(2)}) async-start(), calls=%async_computation.51 | async-start | bytes 12976128 | tf_op jit(solution)/shard_map/reduce_scatter | solution.py:414
  1542.1 1686.3 %reduce-scatter.51.cloned.1.call-start = ((), (), s32[]{:S(2)}) async-start(), calls=%async_computation.50 | async-start | bytes 12976128 | tf_op jit(solution)/shard_map/reduce_scatter | solution.py:414
  1550.0 1841.1 %reduce-scatter.43.cloned.1.call-start = ((), (), s32[]{:S(2)}) async-start(), calls=%async_computation.46 | async-start | bytes 12976128 | tf_op jit(solution)/shard_map/reduce_scatter | solution.py:408
  1557.8 1995.9 %reduce-scatter.47.cloned.1.call-start = ((), (), s32[]{:S(2)}) async-start(), calls=%async_computation.48 | async-start | bytes 12976128 | tf_op jit(solution)/shard_map/reduce_scatter | solution.py:411
  1565.5 2140.9 %all-reduce.14.cloned.1.call-start = ((), (), s32[]{:S(2)}) async-start(), calls=%async_computation.66 | async-start | bytes 6488064 | tf_op jit(solution)/shard_map/psum | solution.py:420
  (170 other events, 7733.1 us)
Sparse Core Ops, SparseCore 0:
  10.3 60.3 all-gather.34
  73.0 57.2 all-gather.32
  132.5 64.7 all-gather.36
  198.9 65.1 all-gather.38
  265.6 75.6 all-gather.40
  342.9 76.9 all-gather.42
  421.6 76.9 all-gather.44
  500.3 61.6 all-gather.50
  563.6 57.3 all-gather.48
  622.5 57.1 all-gather.46
  681.4 86.5 all-gather.58
  769.6 61.7 all-gather.52
  833.1 75.8 all-gather.56
  910.6 76.9 all-gather.54
  1116.2 65.0 reduce-scatter.18
  1184.1 29.4 reduce-scatter.20
  1375.1 66.0 reduce-scatter.22
  1475.8 135.3 reduce-scatter.32
  1613.4 132.4 reduce-scatter.36
  1748.4 132.2 reduce-scatter.30
  1883.0 132.2 reduce-scatter.34
  2017.8 138.6 reduce-scatter.40
  2158.7 139.3 reduce-scatter.28
  2300.5 138.8 reduce-scatter.38
  2441.6 139.0 reduce-scatter.26
  2583.0 158.1 reduce-scatter.44
  2743.6 160.2 reduce-scatter.48
  2906.2 159.8 reduce-scatter.52
  3068.4 159.9 reduce-scatter.50
  3230.8 160.3 reduce-scatter.42
  3393.5 160.1 reduce-scatter.46
  3557.0 77.4 all-reduce.13
  (1 shorter events, 29.4 us)
where the time goes:
time: 3740 us; the launch traced here: 3720 us
  waiting for transfers between devices  2700 us (72%)
  blocking collectives  380 us (10%)
  matrix products  245 us (7%)
  local copies, waits for them, and re-layouts  201 us (5%)
  other arithmetic  122 us (3%)
  starting transfers between devices  51.2 us (1%)
    reduce_scatter x2, waiting for transfers between devices, reduce_grads(): lax.psum_scatter(grads[7].astype(jnp.bfloat16), ('dp', 'ctx'), scatter_di...  325 us
    reduce_scatter x2, waiting for transfers between devices, reduce_grads(): lax.psum_scatter(grads[8].astype(jnp.bfloat16), ('dp', 'ctx'), scatter_di...  325 us
    reduce_scatter x2, waiting for transfers between devices, reduce_grads(): lax.psum_scatter(grads[6].astype(jnp.bfloat16), ('dp', 'ctx'), scatter_di...  323 us
    reduce_scatter x2, waiting for transfers between devices, reduce_grads(): lax.psum_scatter(grads[1].astype(jnp.bfloat16), ('dp', 'ctx'), scatter_di...  283 us
    reduce_scatter x2, waiting for transfers between devices, reduce_grads(): lax.psum_scatter(grads[4].astype(jnp.bfloat16), ('dp', 'ctx'), scatter_di...  282 us
    reduce_scatter x2, waiting for transfers between devices, reduce_grads(): lax.psum_scatter(grads[3].astype(jnp.bfloat16), ('dp', 'ctx'), scatter_di...  269 us
    unnamed x2, blocking collectives  257 us
    reduce_scatter x2, waiting for transfers between devices, reduce_grads(): lax.psum_scatter(grads[2].astype(jnp.bfloat16), ('dp', 'ctx'), scatter_di...  180 us
  transfers between devices with their start and end apart: 44, of which 32 were waited for; matrix products, arithmetic and copies ran while one was open for 8% of the time, Pallas kernels for 0%

commit v1 on v0

v1 whole, which is shorter than its diff:
```python
import functools

import jax
import jax.numpy as jnp
from jax import lax
from jax.experimental import pallas as pl
from jax.experimental.pallas import tpu as pltpu
from jax.sharding import PartitionSpec as P

HEAD = 96
LAYERS = 2
D = 1536
EPS = 1e-05
BASE = 100000.0
NEG = -1e30
F32 = jnp.float32
BF = jnp.bfloat16
MESH = pl.DeviceIdType.MESH
VMEM_LIMIT = 56 * 1024 * 1024


def place():
    dp, ctx, head = lax.axis_index("dp"), lax.axis_index("ctx"), lax.axis_index("head")
    y, zlo = lax.div(dp, 2), lax.rem(dp, 2)
    zhi, core = lax.div(ctx, 2), lax.rem(ctx, 2)
    return dict(dp=dp, ctx=ctx, x=head, y=y, zlo=zlo, zhi=zhi, core=core, z=zhi * 2 + zlo)


def dev(p, dx=0, dy=0, dz=0, dc=0):
    x = lax.rem(p["x"] + dx, 4)
    y = lax.rem(p["y"] + dy, 4)
    z = lax.rem(p["z"] + dz, 4)
    core = lax.rem(p["core"] + dc, 2)
    return (y * 2 + lax.rem(z, 2), lax.div(z, 2) * 2 + core, x)


def z_slot(z):
    return lax.rem(z, 2) * 2 + lax.div(z, 2)


class Op:
    def __init__(self, ins, outs, scratch, offsets, run, alias=()):
        self.ins, self.outs, self.scratch = list(ins), list(outs), list(scratch)
        self.offsets, self.run, self.alias = offsets, run, dict(alias)


def sems(n):
    return pltpu.SemaphoreType.DMA((n,))


def build(cid, ops, cost=0):
    ins = [a for op in ops for a in op.ins]
    outs = [o for op in ops for o in op.outs]
    scratch = [s for op in ops for s in op.scratch]
    offsets, alias, i0, o0 = [], {}, 0, 0
    for op in ops:
        for o in op.offsets:
            key = tuple(o.get(k, 0) for k in ("dx", "dy", "dz", "dc"))
            if key not in offsets:
                offsets.append(key)
        for i, o in op.alias.items():
            alias[i0 + i] = o0 + o
        i0, o0 = i0 + len(op.ins), o0 + len(op.outs)
    n_in, n_out = len(ins), len(outs)

    def kernel(*refs):
        p = place()
        if offsets:
            barrier = pltpu.get_barrier_semaphore()
            for o in offsets:
                pl.semaphore_signal(barrier, inc=1, device_id=dev(p, *o), device_id_type=MESH)
            pl.semaphore_wait(barrier, len(offsets))
        i, o, s = 0, n_in, n_in + n_out
        runs = []
        for op in ops:
            runs.append(
                op.run(
                    p,
                    refs[i : i + len(op.ins)],
                    refs[o : o + len(op.outs)],
                    refs[s : s + len(op.scratch)],
                )
            )
            i, o, s = i + len(op.ins), o + len(op.outs), s + len(op.scratch)
        while runs:
            live = []
            for r in runs:
                try:
                    next(r)
                    live.append(r)
                except StopIteration:
                    pass
            runs = live

    results = pl.pallas_call(
        kernel,
        out_shape=[jax.ShapeDtypeStruct(s, d) for s, d in outs],
        in_specs=[pl.BlockSpec(memory_space=pl.ANY)] * n_in,
        out_specs=[pl.BlockSpec(memory_space=pl.ANY)] * n_out,
        scratch_shapes=scratch,
        input_output_aliases=alias,
        compiler_params=pltpu.CompilerParams(
            collective_id=cid, has_side_effects=True, vmem_limit_bytes=VMEM_LIMIT
        ),
    )(*ins)
    split = []
    for op in ops:
        split.append(list(results[: len(op.outs)]))
        results = results[len(op.outs) :]
    return split


def send(src, dst, send_sem, recv_sem, target):
    c = pltpu.make_async_remote_copy(
        src_ref=src,
        dst_ref=dst,
        send_sem=send_sem,
        recv_sem=recv_sem,
        device_id=target,
        device_id_type=MESH,
    )
    c.start()
    return c


def copy(src, dst, sem):
    c = pltpu.make_async_copy(src, dst, sem)
    c.start()
    return c


X_OFF = [dict(dx=d) for d in (1, 3, 2)]
Y_OFF = [dict(dy=d) for d in (1, 3, 2)]
Z_OFF = [dict(dz=d) for d in (1, 3, 2)]
CORE_OFF = [dict(dc=1)]
CTX_OFF = [dict(dz=2, dc=0), dict(dz=2, dc=1), dict(dz=0, dc=1)]
SEQ_OFF = [
    dict(dx=dx, dz=dz, dc=dc) for dx in range(4) for dz in (0, 2) for dc in (0, 1)
][1:]
SHARD_OFF = [
    dict(dy=dy, dz=dz, dc=dc) for dy in range(4) for dz in range(4) for dc in (0, 1)
][1:]


def swap_op(a, out, offsets, near, far):
    block = jax.eval_shape(
        lambda v: near(dict(ctx=0, x=0, core=0, zhi=0), _Shape(v), _Shape(v))[0].value, a
    )
    n = len(offsets)

    def run(p, ins, outs, scratch):
        hold, s, r, k = scratch
        own, spot = near(p, ins[0], outs[0])
        inward = copy(own, hold, k.at[0])
        copies = []
        for i, o in enumerate(offsets):
            t = dev(p, **o)
            src, dst = far(p, ins[0], outs[0], t)
            copies.append(send(src, dst, s.at[i], r.at[i], t))
        yield
        inward.wait()
        outward = copy(hold, spot, k.at[1])
        yield
        outward.wait()
        for c in copies:
            c.wait()

    return Op(
        [a], [out], [pltpu.VMEM(block.shape, block.dtype), sems(n), sems(n), sems(2)], offsets, run
    )


class _Shape:
    def __init__(self, value):
        self.value = value

    @property
    def at(self):
        return self

    def __getitem__(self, index):
        return _Shape(self.value[index])


def gather_x(a):
    out = ((2, 4) + a.shape[1:], a.dtype)

    def near(p, i, o):
        return i, (o.at[:, p["x"]] if not isinstance(o, _Shape) else None)

    return swap_op(a, out, X_OFF, near, lambda p, i, o, t: (i, o.at[:, p["x"]]))


def scatter_x(a):
    out = ((4, 2) + a.shape[2:], a.dtype)
    return swap_op(
        a,
        out,
        X_OFF,
        lambda p, i, o: (i.at[:, p["x"]], o.at[p["x"]]),
        lambda p, i, o, t: (i.at[:, t[2]], o.at[p["x"]]),
    )


def swap_ctx(a):
    return swap_op(
        a,
        (a.shape, a.dtype),
        CTX_OFF,
        lambda p, i, o: (i.at[p["ctx"]], o.at[p["ctx"]]),
        lambda p, i, o, t: (i.at[t[1]], o.at[p["ctx"]]),
    )


def heads_to_tokens(a):
    return swap_op(
        a,
        ((4, 2, 2) + a.shape[2:], a.dtype),
        SEQ_OFF,
        lambda p, i, o: (
            i.at[p["ctx"], p["x"]],
            None if isinstance(o, _Shape) else o.at[p["x"], p["core"], p["zhi"]],
        ),
        lambda p, i, o, t: (i.at[t[1], t[2]], o.at[p["x"], p["core"], p["zhi"]]),
    )


def tokens_to_heads(a):
    return swap_op(
        a,
        ((4, 4) + a.shape[3:], a.dtype),
        SEQ_OFF,
        lambda p, i, o: (
            i.at[p["x"], p["core"], p["zhi"]],
            None if isinstance(o, _Shape) else o.at[p["ctx"], p["x"]],
        ),
        lambda p, i, o, t: (
            i.at[t[2], lax.rem(t[1], 2), lax.div(t[1], 2)],
            o.at[p["ctx"], p["x"]],
        ),
    )


def all_places(a):
    return swap_op(
        a,
        ((4, 4) + a.shape, a.dtype),
        SEQ_OFF,
        lambda p, i, o: (i, None if isinstance(o, _Shape) else o.at[p["ctx"], p["x"]]),
        lambda p, i, o, t: (i, o.at[p["ctx"], p["x"]]),
    )


def all_shards(a):
    return swap_op(
        a,
        ((8, 4) + a.shape, a.dtype),
        SHARD_OFF,
        lambda p, i, o: (i, None if isinstance(o, _Shape) else o.at[p["dp"], p["ctx"]]),
        lambda p, i, o, t: (i, o.at[p["dp"], p["ctx"]]),
    )


def line_off(axis, which=(1, 3, 2)):
    return [{"d" + axis: d} for d in which]


def ag_first(shard, order):
    whole = ((4, 4, 2) + shard.shape, shard.dtype)

    def run(p, ins, outs, scratch):
        hold, s, r, k = scratch
        dst = outs[0].at[p["y"], z_slot(p["z"]), p["core"]]
        inward = copy(ins[0], hold, k.at[0])
        copies = [
            send(ins[0], dst, s.at[i], r.at[i], dev(p, **o))
            for i, o in enumerate(line_off(order[0]))
        ]
        yield
        inward.wait()
        outward = copy(hold, dst, k.at[1])
        yield
        outward.wait()
        for c in copies:
            c.wait()

    return Op(
        [shard],
        [whole],
        [pltpu.VMEM(shard.shape, shard.dtype), sems(3), sems(3), sems(2)],
        line_off(order[0]),
        run,
    )


def ag_second(whole, order, which=(1, 3, 2)):
    def run(p, ins, outs, scratch):
        s, r = scratch
        if order == "zy":
            block = outs[0].at[p["y"], :, p["core"]]
        else:
            block = outs[0].at[:, z_slot(p["z"]), p["core"]]
        copies = [
            send(block, block, s.at[i], r.at[i], dev(p, **o))
            for i, o in enumerate(line_off(order[1], which))
        ]
        yield
        yield
        for c in copies:
            c.wait()

    n = len(which)
    return Op(
        [whole],
        [(whole.shape, whole.dtype)],
        [sems(n), sems(n)],
        line_off(order[1], which),
        run,
        {0: 0},
    )


def ag_third(whole):
    def run(p, ins, outs, scratch):
        s, r = scratch
        block = outs[0].at[:, :, p["core"]]
        c = send(block, block, s.at[0], r.at[0], dev(p, dc=1))
        yield
        yield
        c.wait()

    return Op([whole], [(whole.shape, whole.dtype)], [sems(1), sems(1)], CORE_OFF, run, {0: 0})


def ag_all(shard, order):
    first = ag_first(shard, order)

    def run(p, ins, outs, scratch):
        yield from first.run(p, ins, outs, scratch[:4])
        yield from ag_second(jax.ShapeDtypeStruct(*first.outs[0]), order).run(
            p, outs, outs, scratch[4:6]
        )
        yield
        yield from ag_third(jax.ShapeDtypeStruct(*first.outs[0])).run(p, outs, outs, scratch[6:8])

    return Op(
        [shard],
        first.outs,
        first.scratch + [sems(3), sems(3), sems(1), sems(1)],
        first.offsets + line_off(order[1]) + CORE_OFF,
        run,
    )


def ag_rest(whole, order):
    second, third = ag_second(whole, order), ag_third(whole)

    def run(p, ins, outs, scratch):
        yield from second.run(p, ins, outs, scratch[:2])
        yield
        yield from third.run(p, ins, outs, scratch[2:])

    return Op(
        [whole],
        second.outs,
        second.scratch + third.scratch,
        second.offsets + CORE_OFF,
        run,
        {0: 0},
    )


def rs_cross(g):
    def run(p, ins, outs, scratch):
        s, r = scratch
        c = send(ins[0].at[:, :, 1 - p["core"]], outs[0], s.at[0], r.at[0], dev(p, dc=1))
        yield
        yield
        c.wait()

    return Op([g], [((4, 4) + g.shape[3:], g.dtype)], [sems(1), sems(1)], CORE_OFF, run)


def add_into(dst, terms, rows):
    def body(k, carry):
        at = pl.ds(pl.multiple_of(k * 16, 16), 16)
        for n in range(dst.shape[0]):
            total = terms[0][n, at].astype(F32)
            for t in terms[1:]:
                total = total + t[n, at].astype(F32)
            dst[n, at] = total.astype(BF)
        return carry

    lax.fori_loop(0, rows // 16, body, 0)


def along(p, axis, d):
    return lax.rem(p["y"] + d, 4) if axis == "y" else z_slot(lax.rem(p["z"] + d, 4))


def rs_line(g, crossed, order):
    rows, cols = g.shape[3:]
    chunk = (4, rows, cols)

    def run(p, ins, outs, scratch):
        mine, other, got, load, s, r, k = scratch
        loads = []
        for d in (1, 3, 2, 0):
            at = along(p, order[0], d)
            if order[0] == "y":
                a, b = ins[0].at[at, :, p["core"]], ins[1].at[at]
            else:
                a, b = ins[0].at[:, at, p["core"]], ins[1].at[:, at]
            loads.append(
                (d, copy(a, mine.at[d], load.at[d]), copy(b, other.at[d], load.at[4 + d]))
            )
        yield
        copies = []
        for d, a, b in loads:
            a.wait()
            b.wait()
            add_into(mine.at[d], [mine.at[d], other.at[d]], rows)
            if d:
                copies.append(
                    send(
                        mine.at[d],
                        got.at[d - 1],
                        s.at[d - 1],
                        r.at[d - 1],
                        dev(p, **{"d" + order[0]: d}),
                    )
                )
        yield
        yield
        for c in copies:
            c.wait()
        add_into(other.at[0], [mine.at[0], got.at[0], got.at[1], got.at[2]], rows)
        out = copy(other.at[0], outs[0], k.at[0])
        yield
        out.wait()

    return Op(
        [g, crossed],
        [(chunk, BF)],
        [
            pltpu.VMEM((4,) + chunk, BF),
            pltpu.VMEM((4,) + chunk, BF),
            pltpu.VMEM((3,) + chunk, BF),
            sems(8),
            sems(3),
            sems(3),
            sems(1),
        ],
        line_off(order[0]),
        run,
    )


def rs_last(part, order):
    rows, cols = part.shape[1:]

    def run(p, ins, outs, scratch):
        own, got, total, k, s, r, sx, rx = scratch
        load = copy(ins[0].at[pl.ds(along(p, order[1], 0), 1)], own, k.at[0])
        copies = []
        for i, o in enumerate(line_off(order[1])):
            d = o["d" + order[1]]
            copies.append(
                send(
                    ins[0].at[pl.ds(along(p, order[1], d), 1)],
                    got.at[i],
                    s.at[i],
                    r.at[i],
                    dev(p, **o),
                )
            )
        yield
        load.wait()
        yield
        for c in copies:
            c.wait()
        add_into(total, [own, got.at[0], got.at[1], got.at[2]], rows)
        dst = outs[0].at[pl.ds(p["x"], 1)]
        near = copy(total, dst, k.at[1])
        copies = [
            send(total, dst, sx.at[i], rx.at[i], dev(p, **o)) for i, o in enumerate(X_OFF)
        ]
        yield
        near.wait()
        for c in copies:
            c.wait()

    one = (1, rows, cols)
    return Op(
        [part],
        [((4, rows, cols), BF)],
        [
            pltpu.VMEM(one, BF),
            pltpu.VMEM((3,) + one, BF),
            pltpu.VMEM(one, BF),
            sems(2),
            sems(3),
            sems(3),
            sems(3),
            sems(3),
        ],
        line_off(order[1]) + X_OFF,
        run,
    )


def sum_all(a):
    shape = a.shape
    axes = ("dx", "dy", "dz")

    def run(p, ins, outs, scratch):
        acc, got, k, s, r = scratch
        copy(ins[0], acc.at[0], k.at[0]).wait()
        for n, axis in enumerate(axes):
            copies = [
                send(
                    acc.at[n],
                    got.at[3 * n + d - 1],
                    s.at[3 * n + d - 1],
                    r.at[3 * n + d - 1],
                    dev(p, **{axis: d}),
                )
                for d in (1, 2, 3)
            ]
            yield
            for c in copies:
                c.wait()
            acc[n + 1] = acc[n] + got[3 * n] + got[3 * n + 1] + got[3 * n + 2]
        c = send(acc.at[3], got.at[9], s.at[9], r.at[9], dev(p, dc=1))
        yield
        c.wait()
        acc[4] = acc[3] + got[9]
        copy(acc.at[4], outs[0], k.at[0]).wait()

    return Op(
        [a],
        [(shape, F32)],
        [pltpu.VMEM((5,) + shape, F32), pltpu.VMEM((10,) + shape, F32), sems(1), sems(10), sems(10)],
        X_OFF + Y_OFF + Z_OFF + CORE_OFF,
        run,
    )


def pick(a, index, axis):
    return lax.dynamic_index_in_dim(a, index, axis, keepdims=False)


def rotated(y, cosine, sine):
    lane = lax.broadcasted_iota(jnp.int32, y.shape, 1)
    low = lax.rem(lane, HEAD) < HEAD // 2
    width = y.shape[1]
    turned = jnp.where(low, pltpu.roll(y, width - HEAD // 2, 1), pltpu.roll(y, HEAD // 2, 1))
    return y * cosine + turned * sine


def qkv_kernel(x_ref, w_ref, cos_ref, sin_ref, o_ref):
    for u in range(2):
        for s in range(2):
            rows = pl.ds(s * 256, 256)
            y = jnp.dot(
                x_ref[rows], w_ref[:, u * 384 : (u + 1) * 384], preferred_element_type=F32
            )
            o_ref[s * 2 + u] = rotated(y, cos_ref[rows], sin_ref[rows]).astype(BF)


def project(x, w, cosine, sine):
    return pl.pallas_call(
        qkv_kernel,
        out_shape=jax.ShapeDtypeStruct((4, 256, 384), BF),
        compiler_params=pltpu.CompilerParams(vmem_limit_bytes=VMEM_LIMIT),
        cost_estimate=pl.CostEstimate(flops=1208 * 10**6, bytes_accessed=6 * 10**6, transcendentals=0),
    )(x, w, cosine, sine)


def contract(a, b, da, db):
    return lax.dot_general(a, b, (((da,), (db,)), ((), ())), preferred_element_type=F32)


SCALE = HEAD ** (-0.5)


def masked(st, i):
    width = st.shape[0]
    key = lax.broadcasted_iota(jnp.int32, (256, 256), 0)
    query = lax.broadcasted_iota(jnp.int32, (256, 256), 1)
    last = jnp.where(key <= query, st[width - 256 :], NEG)
    return last if width == 256 else jnp.concatenate([st[: width - 256], last], axis=0)


def attend_kernel(qkv_ref, o_ref, lse_ref):
    for i in range(4):
        rows = pl.ds(i * 256, 256)
        width = (i + 1) * 256
        k = qkv_ref[:width, 2 * HEAD : 3 * HEAD]
        v = qkv_ref[:width, 3 * HEAD : 4 * HEAD]
        outs = []
        for n in range(2):
            q = qkv_ref[rows, n * HEAD : (n + 1) * HEAD]
            st = masked(contract(k, q, 1, 1) * SCALE, i)
            top = jnp.max(st, axis=0, keepdims=True)
            e = jnp.exp(st - top)
            total = jnp.sum(e, axis=0, keepdims=True)
            ot = contract(v, e.astype(BF), 0, 0)
            outs.append(ot * (1.0 / total))
            lse_ref[n : n + 1, rows] = top + jnp.log(total)
        o_ref[rows] = jnp.concatenate(outs, axis=0).T.astype(BF)


def attend(qkv):
    return pl.pallas_call(
        attend_kernel,
        out_shape=[jax.ShapeDtypeStruct((1024, 192), BF), jax.ShapeDtypeStruct((2, 1024), F32)],
        compiler_params=pltpu.CompilerParams(vmem_limit_bytes=VMEM_LIMIT),
        cost_estimate=pl.CostEstimate(flops=10**9, bytes_accessed=10**6, transcendentals=1310720),
    )(qkv)


def attend_back_kernel(qkv_ref, do_ref, lse_ref, cos_ref, sin_ref, o_ref, dq_ref, dk_ref, dv_ref):
    dk_ref[...] = jnp.zeros_like(dk_ref)
    dv_ref[...] = jnp.zeros_like(dv_ref)
    for i in range(4):
        rows = pl.ds(i * 256, 256)
        width = (i + 1) * 256
        k = qkv_ref[:width, 2 * HEAD : 3 * HEAD]
        v = qkv_ref[:width, 3 * HEAD : 4 * HEAD]
        for n in range(2):
            q = qkv_ref[rows, n * HEAD : (n + 1) * HEAD]
            do = do_ref[rows, n * HEAD : (n + 1) * HEAD]
            st = masked(contract(k, q, 1, 1) * SCALE, i)
            p = jnp.exp(st - lse_ref[n : n + 1, rows])
            dpt = contract(v, do, 1, 1)
            delta = jnp.sum(p * dpt, axis=0, keepdims=True)
            ds = (p * (dpt - delta)).astype(BF)
            dq_ref[n * HEAD : (n + 1) * HEAD, rows] = contract(k, ds, 0, 0)
            dk_ref[:width] += jnp.dot(ds, q, preferred_element_type=F32)
            dv_ref[:width] += jnp.dot(p.astype(BF), do, preferred_element_type=F32)
    for i in range(4):
        rows = pl.ds(i * 256, 256)
        g = jnp.concatenate(
            [dq_ref[:, rows].T * SCALE, dk_ref[rows] * SCALE, dv_ref[rows]], axis=1
        )
        g = g.astype(BF).astype(F32)
        o_ref[rows] = rotated(g, cos_ref[rows], -sin_ref[rows]).astype(BF)


def attend_back(qkv, do, lse, cosine, sine):
    return pl.pallas_call(
        attend_back_kernel,
        out_shape=jax.ShapeDtypeStruct((1024, 384), BF),
        scratch_shapes=[
            pltpu.VMEM((192, 1024), F32),
            pltpu.VMEM((1024, HEAD), F32),
            pltpu.VMEM((1024, HEAD), F32),
        ],
        compiler_params=pltpu.CompilerParams(vmem_limit_bytes=VMEM_LIMIT),
        cost_estimate=pl.CostEstimate(flops=3 * 10**9, bytes_accessed=10**6, transcendentals=1310720),
    )(qkv, do, lse, cosine, sine)


def out_kernel(m_ref, w_ref, hidden_ref, gain_ref, res_ref, norm_ref, scale_ref, tok_ref):
    tok_ref[...] = jnp.concatenate([m_ref[g] for g in range(8)], axis=1)
    for c in range(3):
        cols = slice(c * 512, (c + 1) * 512)
        res_ref[:, cols] = hidden_ref[:, cols] + jnp.dot(
            tok_ref[...], w_ref[:, cols], preferred_element_type=F32
        )
    res = res_ref[...]
    scale = lax.rsqrt(jnp.mean(res * res, axis=-1, keepdims=True) + EPS)
    scale_ref[...] = scale
    norm_ref[...] = (res * scale * gain_ref[...]).astype(BF)


def out_project(m, w, hidden, gain):
    return pl.pallas_call(
        out_kernel,
        out_shape=[
            jax.ShapeDtypeStruct((128, D), F32),
            jax.ShapeDtypeStruct((128, D), BF),
            jax.ShapeDtypeStruct((128, 1), F32),
            jax.ShapeDtypeStruct((128, D), BF),
        ],
        compiler_params=pltpu.CompilerParams(vmem_limit_bytes=VMEM_LIMIT),
        cost_estimate=pl.CostEstimate(flops=604 * 10**6, bytes_accessed=7 * 10**6, transcendentals=0),
    )(m, w, hidden, gain)


def rope_columns(positions):
    half = HEAD // 2
    frequency = BASE ** (-(jnp.arange(half, dtype=F32) * 2.0 / HEAD))
    angles = positions.astype(F32)[:, None] * frequency
    cosine, sine = jnp.cos(angles), jnp.sin(angles)
    one, zero = jnp.ones_like(cosine), jnp.zeros_like(sine)
    return (
        jnp.concatenate([cosine] * 6 + [one] * 2, axis=1),
        jnp.concatenate([-sine, sine] * 3 + [zero] * 2, axis=1),
    )


def norm(hidden, gain):
    scale = lax.rsqrt(jnp.mean(hidden * hidden, axis=-1, keepdims=True) + EPS)
    return (hidden * scale * gain).astype(BF), scale


def norm_back(hidden, scale, gain, upstream):
    unit = hidden * scale
    gain_grad = jnp.sum(upstream * unit, axis=0)
    weighted = upstream * gain
    return (
        scale * (weighted - unit * jnp.mean(weighted * unit, axis=-1, keepdims=True)),
        gain_grad,
    )


def dot(a, b):
    return jnp.dot(a, b, preferred_element_type=F32)


def dot_t(a, b):
    return contract(a, b, 1, 1)


def t_dot(a, b):
    return contract(a, b, 0, 0)


def ff_quarter(a, x):
    rows = a.shape[0]
    return pick(a.reshape(rows, 32, 4, 32), x, 2).reshape(rows, 1024)


def pack_qkv(q, k, v, x):
    rows = q.shape[0]
    q = lax.dynamic_slice_in_dim(q, x * 384, 384, 1).reshape(rows, 2, 192)
    k = lax.dynamic_slice_in_dim(k, x * 192, 192, 1).reshape(rows, 2, 96)
    v = lax.dynamic_slice_in_dim(v, x * 192, 192, 1).reshape(rows, 2, 96)
    return jnp.concatenate([q, k, v], axis=2).reshape(rows, 768)


def per_device(
    inputs,
    positions,
    cotangent,
    attn_gain,
    query_weight,
    key_matrix,
    value_matrix,
    out_weight,
    mlp_gain,
    gate_weight,
    up_weight,
    down_weight,
):
    p = place()
    x = p["x"]

    shards = []
    for l in range(LAYERS):
        gu = jnp.concatenate([ff_quarter(gate_weight[l], x), ff_quarter(up_weight[l], x)], axis=1)
        down = lax.dynamic_slice_in_dim(down_weight[l], x * 32, 32, 0)
        qkv = pack_qkv(query_weight[l], key_matrix[l], value_matrix[l], x)
        shards.append((qkv, out_weight[l], down, gu))
    orders = ("zy", "yz", "yz", "zy")

    gains = jnp.zeros((8, 128), F32)
    gains = gains.at[:2, :48].set(attn_gain.astype(F32)).at[2:4, :48].set(mlp_gain.astype(F32))
    places = jnp.broadcast_to(positions.reshape(1, 128), (8, 128))
    first = build(
        1,
        [gather_x(inputs), all_places(places), all_shards(gains)]
        + [ag_all(s, o) for s, o in zip(shards[0], orders)],
    )
    ((tokens_g,), (places_g,), (gains_g,)) = first[:3]
    whole = [[w[0] for w in first[3:]], None]
    gains_all = gains_g.reshape(32, 8, 128)[:, :4, :48].transpose(1, 0, 2).reshape(4, 1, D)
    place_all = places_g[:, :, 0, :].reshape(4, 4, 2, 64)
    cos_c, sin_c = rope_columns(pick(place_all, p["ctx"], 0).transpose(1, 0, 2).reshape(512))
    cos_s, sin_s = rope_columns(pick(place_all, p["zhi"], 2).reshape(1024))

    def stage(ws, order_list, f):
        return [f(w, o) for w, o in zip(ws, order_list)]

    hidden = inputs.reshape(128, D).astype(F32)
    saved = []
    for l in range(LAYERS):
        if l == 0:
            normed_g, _ = norm(tokens_g.reshape(512, D).astype(F32), gains_all[0])
            scale_one = lax.rsqrt(jnp.mean(hidden * hidden, axis=-1, keepdims=True) + EPS)
        else:
            normed, scale_one = norm(hidden, gains_all[l])
            (ng,), *rest = build(
                2,
                [gather_x(normed.reshape(2, 64, D))]
                + [ag_second(w, o, (2,)) for w, o in zip(whole[1][1:], orders[1:])],
            )
            whole[1][1:] = [w[0] for w in rest]
            normed_g = ng.reshape(512, D)
        w_qkv = whole[l][0].reshape(D, 768)
        units = project(normed_g, w_qkv, cos_c, sin_c)
        if l == 0:
            ((qkv,),) = build(3, [swap_ctx(units)])
        else:
            (qkv,), *rest = build(4, [swap_ctx(units)] + [ag_third(w) for w in whole[1][1:]])
            whole[1][1:] = [w[0] for w in rest]
        qkv = qkv.reshape(1024, 384)
        mixed, lse = attend(qkv)
        ((mixed_t,),) = build(5, [heads_to_tokens(mixed.reshape(4, 4, 64, 192))])
        w_out, w_down, w_gu = whole[l][1:]
        w_out, w_down, w_gu = w_out.reshape(D, D), w_down.reshape(1024, D), w_gu.reshape(D, 2048)
        residual, normed_two, scale_two, mixed_tok = out_project(
            mixed_t.reshape(8, 128, 192), w_out, hidden, gains_all[2 + l]
        )
        fg = gather_x(normed_two.reshape(2, 64, D))
        if l == 0:
            (ng,), *rest = build(6, [fg] + [ag_first(s, o) for s, o in zip(shards[1], orders)])
            whole[1] = [w[0] for w in rest]
        else:
            ((ng,),) = build(7, [fg])
        normed_two_g = ng.reshape(512, D)
        gate_up = dot(normed_two_g, w_gu)
        gate, up = gate_up[:, :1024], gate_up[:, 1024:]
        activ = (jax.nn.silu(gate) * up).astype(BF)
        partial = dot(activ, w_down).astype(BF)
        fg = scatter_x(partial.reshape(2, 4, 64, D))
        if l == 0:
            (terms,), *rest = build(
                8,
                [fg, ag_rest(whole[1][0], "zy")]
                + [ag_second(w, o, (1, 3)) for w, o in zip(whole[1][1:], orders[1:])],
            )
            whole[1] = [w[0] for w in rest]
        else:
            ((terms,),) = build(9, [fg])
        saved.append(
            (
                hidden, normed_g, scale_one, qkv, lse, mixed_tok, residual, normed_two_g, scale_two,
                gate_up, activ, w_qkv, w_out, w_down, w_gu,
            )
        )
        hidden = residual + jnp.sum(terms.astype(F32), axis=0).reshape(128, D)
    output = hidden.astype(BF).reshape(2, 64, D)

    gradient = cotangent.reshape(128, D).astype(F32)
    ends = [[None] * 4 for _ in range(LAYERS)]
    gain_grads = [None] * 4
    later = None
    for l in reversed(range(LAYERS)):
        (
            hidden, normed_g, scale_one, qkv, lse, mixed_tok, residual, normed_two_g, scale_two,
            gate_up, activ, w_qkv, w_out, w_down, w_gu,
        ) = saved[l]
        grad_b = cotangent if l == LAYERS - 1 else gradient.astype(BF).reshape(2, 64, D)
        fg = gather_x(grad_b)
        if l == 1:
            ((gb,),) = build(7, [fg])
        else:
            g_out1, c_out1, g_qkv1, part_gu1, part_down1 = later
            (gb,), (part_out1,), (c_qkv1,) = build(
                10, [fg, rs_line(g_out1, c_out1, "yz"), rs_cross(g_qkv1)]
            )
        grad_b_g = gb.reshape(512, D)
        grad_act = dot_t(grad_b_g, w_down)
        gate, up = gate_up[:, :1024], gate_up[:, 1024:]
        sigma = jax.nn.sigmoid(gate)
        grad_gate = (grad_act * up * sigma * (1.0 + gate * (1.0 - sigma))).astype(BF)
        grad_up = (grad_act * gate * sigma).astype(BF)
        grad_gu = jnp.concatenate([grad_gate, grad_up], axis=1)
        partial = dot_t(grad_gu, w_gu).astype(BF)
        fg = scatter_x(partial.reshape(2, 4, 64, D))
        if l == 1:
            ((terms,),) = build(9, [fg])
        else:
            (terms,), (part_qkv1,), (ends[1][2],) = build(
                11, [fg, rs_line(g_qkv1, c_qkv1, "zy"), rs_last(part_down1, "yz")]
            )
        g_down = t_dot(activ, grad_b_g).astype(BF).reshape(4, 4, 2, 32, D)
        g_gu = t_dot(normed_two_g, grad_gu).astype(BF).reshape(4, 4, 2, 48, 2048)
        grad_normed = jnp.sum(terms.astype(F32), axis=0).reshape(128, D)
        back, gain_grads[2 + l] = norm_back(residual, scale_two, gains_all[2 + l], grad_normed)
        grad_res = gradient + back
        grad_rb = grad_res.astype(BF)
        grad_mix = dot_t(grad_rb, w_out).astype(BF)
        grad_mix = grad_mix.reshape(128, 8, 192).transpose(1, 0, 2).reshape(4, 2, 2, 64, 192)
        fg = tokens_to_heads(grad_mix)
        if l == 1:
            (gm,), (c_down,), (c_gu,) = build(12, [fg, rs_cross(g_down), rs_cross(g_gu)])
        else:
            (gm,), (c_down,), (c_gu,), (ends[1][3],), (ends[1][1],) = build(
                13,
                [fg, rs_cross(g_down), rs_cross(g_gu), rs_last(part_gu1, "zy"), rs_last(part_out1, "yz")],
            )
        g_out = t_dot(mixed_tok, grad_rb).astype(BF).reshape(4, 4, 2, 48, D)
        grad_units = attend_back(qkv, gm.reshape(1024, 192), lse, cos_s, sin_s)
        fg = swap_ctx(grad_units.reshape(4, 256, 384))
        (gu4,), (part_down,), (c_out,) = build(
            14, [fg, rs_line(g_down, c_down, "yz"), rs_cross(g_out)]
        )
        grad_qkv = gu4.reshape(2, 2, 256, 384).transpose(0, 2, 1, 3).reshape(512, 768)
        partial = dot_t(grad_qkv, w_qkv).astype(BF)
        fg = scatter_x(partial.reshape(2, 4, 64, D))
        g_qkv = t_dot(normed_g, grad_qkv).astype(BF).reshape(4, 4, 2, 48, 768)
        if l == 1:
            (terms,), (part_gu,) = build(15, [fg, rs_line(g_gu, c_gu, "zy")])
            later = (g_out, c_out, g_qkv, part_gu, part_down)
        else:
            (terms,), (part_gu,), (c_qkv,) = build(
                16, [fg, rs_line(g_gu, c_gu, "zy"), rs_cross(g_qkv)]
            )
        grad_normed = jnp.sum(terms.astype(F32), axis=0).reshape(128, D)
        back, gain_grads[l] = norm_back(hidden, scale_one, gains_all[l], grad_normed)
        gradient = grad_res + back

    sums = jnp.zeros((8, D), F32).at[:4].set(jnp.stack(gain_grads))
    (part_qkv,), (part_out,), (ends[0][2],), (ends[0][3],), (ends[1][0],), (gain_sum,) = build(
        17,
        [
            rs_line(g_qkv, c_qkv, "zy"),
            rs_line(g_out, c_out, "yz"),
            rs_last(part_down, "yz"),
            rs_last(part_gu, "zy"),
            rs_last(part_qkv1, "zy"),
            sum_all(sums),
        ],
    )
    (ends[0][0],), (ends[0][1],) = build(18, [rs_last(part_qkv, "zy"), rs_last(part_out, "yz")])

    reduced = []
    for l in range(LAYERS):
        a_qkv, s_out, a_down, a_gu = ends[l]
        a_gu = a_gu.reshape(4, 48, 2, 32, 32).transpose(2, 1, 3, 0, 4).reshape(2, 48, 4096).astype(F32)
        a_qkv = a_qkv.reshape(4, 48, 2, 384).transpose(1, 0, 2, 3).astype(F32)
        reduced.append(
            (
                a_qkv[..., :192].reshape(48, D),
                a_qkv[..., 192:288].reshape(48, 768),
                a_qkv[..., 288:].reshape(48, 768),
                jnp.sum(s_out.astype(F32), axis=0),
                a_gu[0],
                a_gu[1],
                a_down.reshape(128, D).astype(F32),
            )
        )

    block = p["dp"] * 4 + p["ctx"]
    gain_own = pick(gain_sum[:4].reshape(4, 32, 48), block, 1)
    stacked = [jnp.stack([reduced[l][k] for l in range(LAYERS)]) for k in range(7)]
    return (
        output,
        gradient.reshape(2, 64, D),
        gain_own[:2],
        stacked[0],
        stacked[1],
        stacked[2],
        stacked[3],
        gain_own[2:],
        stacked[4],
        stacked[5],
        stacked[6],
    )


def solution(mesh):
    tokens = P("dp", ("ctx", "head"), None)
    vector = P(None, ("dp", "ctx"))
    matrix = P(None, ("dp", "ctx"), None)
    return jax.shard_map(
        per_device,
        mesh=mesh,
        in_specs=(
            tokens,
            P("dp", ("ctx", "head")),
            tokens,
            vector,
            matrix,
            matrix,
            matrix,
            matrix,
            vector,
            matrix,
            matrix,
            matrix,
        ),
        out_specs=(
            tokens,
            tokens,
            vector,
            matrix,
            matrix,
            matrix,
            matrix,
            vector,
            matrix,
            matrix,
            matrix,
        ),
        check_vma=False,
    )
```

time: 3740 us -> 894 us (0.24)
  waiting for transfers between devices: 2700 us -> 0 us
  Pallas kernels: 0 us -> 667 us
  blocking collectives: 380 us -> 0 us
  matrix products: 245 us -> 85.5 us
  local copies, waits for them, and re-layouts: 201 us -> 90.6 us
  other arithmetic: 122 us -> 42.6 us
  starting transfers between devices: 51.2 us -> 0 us
    reduce_scatter x18 -> x0, waiting for transfers between devices: 2140 us -> none  [the longest x2 325 us: reduce_grads(): lax.psum_scatter(grads[7].astype(jnp.bfloat16), ('dp', 'ctx'), scatter_di...]
    pallas_call x0 -> x30, Pallas kernels: none -> 667 us  [the longest x22 616 us: build(): pl.pallas_call(kernel, out_shape=[jax.ShapeDtypeStruct(s, d) for s, d in...]
    all_gather x14 -> x0, waiting for transfers between devices: 541 us -> none  [the longest x2 145 us: gather_layer(): lax.all_gather(pieces[7], ('dp', 'ctx'), axis=0, tiled=True)]
    unnamed x2 -> x0, blocking collectives: 257 us -> none
    dot_general x70 -> x20, matrix products: 245 us -> 85.5 us  [the longest x16 66.5 us: contract(): lax.dot_general(a, b, (((da,), (db,)), ((), ())), preferred_element_type=...]
    all_gather x4 -> x0, blocking collectives: 61.3 us -> none  [the longest x2 33.1 us: layer_forward(): lax.all_gather(value_h, 'ctx', axis=1, tiled=True)]
    all_to_all x5 -> x0, blocking collectives: 51.9 us -> none  [the longest x2 19.9 us: layer_backward(): lax.all_to_all(grad_q_b, 'head', split_axis=1, concat_axis=2, tiled=True)]
    all_to_all x11 -> x0, starting transfers between devices: 49.5 us -> none  [the longest x2 10.3 us: layer_forward(): lax.all_to_all(mixed_b, 'head', split_axis=1, concat_axis=2, tiled=True)]
  transfers between devices with their start and end apart: 44 -> 0, of which waited for: 32 -> 0; matrix products, arithmetic and copies ran while one was open for 8% -> 0% of each run, Pallas kernels for 0% -> 0%
where the time goes in v1:
time: 894 us; the launch traced here: 888 us
  Pallas kernels  667 us (75%)
  local copies, waits for them, and re-layouts  90.6 us (10%)
  matrix products  85.5 us (10%)
  other arithmetic  42.6 us (5%)
    pallas_call x22, Pallas kernels, build(): pl.pallas_call(kernel, out_shape=[jax.ShapeDtypeStruct(s, d) for s, d in...  616 us
    dot_general x16, matrix products, contract(): lax.dot_general(a, b, (((da,), (db,)), ((), ())), preferred_element_type=...  66.5 us
    slice x6, local copies, waits for them, and re-layouts, per_device(): a_gu[1]  25.6 us
    dot_general x4, matrix products, dot(): return jnp.dot(a, b, preferred_element_type=F32)  19 us
    pallas_call x2, Pallas kernels, attend_back(): pl.pallas_call(attend_back_kernel, out_shape=jax.ShapeDtypeStruct((1024,...  18.8 us

profile of v1, /device:TPU:0, one launch (start us, length us, event | category | flops | bytes accessed | tf_op | source)
XLA Modules:
  0.0 887.7 jit_solution(17658279783424890896)
XLA Ops:
  11.8 93.4 %shard_map.203 = (bf16[2,4,64,1536]{3,2,1,0:T(8,128)(2,1)}, s32[4,4,8,128]{3,2,1,0:T(8,128)}, f32[8,4,8,128]{3,2,1,0:T(8,128)}, bf16[4,4,2,48,768]{4,3,2,1,0:T(8...) custom-call(bf16[2,64,1536]{2,1,0:T(8,128)(2,1)} %refs_0_.2, ...), custom_call_target="tpu_custom_call" | custom-call | tf_op jit(solution)/shard_map/pallas_call | solution.py:95
  120.7 12.9 %shard_map.205 = bf16[4,256,384]{2,1,0:T(8,128)(2,1)} custom-call(bf16[4,256,384]{2,1,0:T(8,128)(2,1)} %shard_map.204.refs_0_), custom_call_target="tpu_custom_call" | custom-call | tf_op jit(solution)/shard_map/pallas_call | solution.py:95
  133.5 6.0 shard_map.206
  139.5 12.8 %shard_map.207 = bf16[4,2,2,64,192]{4,3,2,1,0:T(8,128)(2,1)} custom-call(bf16[4,4,64,192]{3,2,1,0:T(8,128)(2,1)} %bitcast.298), custom_call_target="tpu_custom_call" | custom-call | tf_op jit(solution)/shard_map/pallas_call | solution.py:95
  161.6 22.9 %shard_map.209 = (bf16[2,4,64,1536]{3,2,1,0:T(8,128)(2,1)}, bf16[4,4,2,48,768]{4,3,2,1,0:T(8,128)(2,1)}, bf16[4,4,2,48,1536]{4,3,2,1,0:T(8,128)(2,1)}, bf16[4,4,...) custom-call(bf16[2,64,1536]{2,1,0:T(8,128)(2,1)} %bitcast.302, bf16[48,768]{1,0:T(8,128)(2,1)} %bitcast.306, ...), custom_call_target="tpu_custom_call" | custom-call | tf_op jit(solution)/shard_map/pallas_call | solution.py:95
  184.5 6.6 fusion.37
  197.8 36.1 %shard_map.210 = (bf16[4,2,64,1536]{3,2,1,0:T(8,128)(2,1)}, bf16[4,4,2,48,768]{4,3,2,1,0:T(8,128)(2,1)}, bf16[4,4,2,48,1536]{4,3,2,1,0:T(8,128)(2,1)}, bf16[4,4,...) custom-call(bf16[2,4,64,1536]{3,2,1,0:T(8,128)(2,1)} %bitcast.265, ...), custom_call_target="tpu_custom_call", output_to_operand_aliasing={{1}: (1, {}), {2}: (2, {}), {3}: (3, {}), {4}: (4, {})} | custom-call | tf_op jit(solution)/shard_map/pallas_call | solution.py:95
  236.9 26.2 %shard_map.211 = (bf16[2,4,64,1536]{3,2,1,0:T(8,128)(2,1)}, bf16[4,4,2,48,1536]{4,3,2,1,0:T(8,128)(2,1)}, bf16[4,4,2,32,1536]{4,3,2,1,0:T(8,128)(2,1)}, bf16[4,4,2,48,2048]{4,3,2,1,0:T(8,128)(2,1)}) custom-call(bf16[2,64,1536]{2,1,0:T(8,128)(2,1)} %bitcast.280, ...), custom_call_target="tpu_custom_call", output_to_operand_aliasing={{1}: (1, {}), {2}: (2, {}), {3}: (3, {})} | custom-call | tf_op jit(solution)/shard_map/pallas_call | solution.py:95
  268.6 13.7 %shard_map.213 = (bf16[4,256,384]{2,1,0:T(8,128)(2,1)}, bf16[4,4,2,48,1536]{4,3,2,1,0:T(8,128)(2,1)}, bf16[4,4,2,32,1536]{4,3,2,1,0:T(8,128)(2,1)}, bf16[4,4,2,48,2048]{4,3,2,1,0:T(8,128)(2,1)}) custom-call(bf16[4,256,384]{2,1,0:T(8,128)(2,1)} %shard_map.212.refs_0_, ...), custom_call_target="tpu_custom_call", output_to_operand_aliasing={{1}: (1, {}), {2}: (2, {}), {3}: (3, {})} | custom-call | tf_op jit(solution)/shard_map/pallas_call | solution.py:95
  282.3 6.1 shard_map.214
  288.3 12.9 %shard_map.215 = bf16[4,2,2,64,192]{4,3,2,1,0:T(8,128)(2,1)} custom-call(bf16[4,4,64,192]{3,2,1,0:T(8,128)(2,1)} %bitcast.299), custom_call_target="tpu_custom_call" | custom-call | tf_op jit(solution)/shard_map/pallas_call | solution.py:95
  306.6 21.5 %shard_map.217 = bf16[2,4,64,1536]{3,2,1,0:T(8,128)(2,1)} custom-call(bf16[2,64,1536]{2,1,0:T(8,128)(2,1)} %bitcast.304), custom_call_target="tpu_custom_call" | custom-call | tf_op jit(solution)/shard_map/pallas_call | solution.py:95
  328.2 6.5 fusion.38
  334.8 20.8 %shard_map.219 = bf16[2,4,64,1536]{3,2,1,0:T(8,128)(2,1)} custom-call(bf16[2,64,1536]{2,1,0:T(8,128)(2,1)} %refs_0_.3), custom_call_target="tpu_custom_call" | custom-call | tf_op jit(solution)/shard_map/pallas_call | solution.py:95
  355.6 7.6 fusion.4
  366.2 19.7 %shard_map.218 = bf16[4,2,64,1536]{3,2,1,0:T(8,128)(2,1)} custom-call(bf16[2,4,64,1536]{3,2,1,0:T(8,128)(2,1)} %bitcast.268), custom_call_target="tpu_custom_call" | custom-call | tf_op jit(solution)/shard_map/pallas_call | solution.py:95
  393.2 18.8 %shard_map.220 = bf16[4,2,64,1536]{3,2,1,0:T(8,128)(2,1)} custom-call(bf16[2,4,64,1536]{3,2,1,0:T(8,128)(2,1)} %bitcast.269), custom_call_target="tpu_custom_call" | custom-call | tf_op jit(solution)/shard_map/pallas_call | solution.py:95
  435.0 13.7 %shard_map.221 = (bf16[4,4,64,192]{3,2,1,0:T(8,128)(2,1)}, bf16[4,4,32,1536]{3,2,1,0:T(8,128)(2,1)}, bf16[4,4,48,2048]{3,2,1,0:T(8,128)(2,1)}) custom-call(bf16[4,2,2,64,192]{4,3,2,1,0:T(8,128)(2,1)} %bitcast.257, bf16[4,4,2,32,1536]{4,3,2,1,0:T(8,128)(2,1)} %bitcast.234, bf16[4,4,2,48,2048]{4,3,2,1,0:T(8,128)(2,1)} %bitcast.226), custom_call_target="tpu_custom_call" | custom-call | tf_op jit(solution)/shard_map/pallas_call | solution.py:95
  460.9 9.4 %shard_map.222 = bf16[1024,384]{1,0:T(8,128)(2,1)} custom-call(bf16[1024,384]{1,0:T(8,128)(2,1)} %bitcast.322, bf16[1024,192]{1,0:T(8,128)(2,1)} %bitcast.323, f32[2,1024]{1,0:T(2,128)} %get-tuple-element.150.lse_ref, f32[1024,384]{1,0:T(8,128)} %concatenate.58.cos_ref, f32[1024,384]{1,0:T(8,128)} %concatenate.60.sin_ref), custom_call_target="tpu_custom_call" | custom-call | flops 3000000000 | bytes 1000000 | tf_op jit(solution)/shard_map/pallas_call | solution.py:652
  470.2 24.0 %shard_map.223 = (bf16[4,256,384]{2,1,0:T(8,128)(2,1)}, bf16[4,32,1536]{2,1,0:T(8,128)(2,1)}, bf16[4,4,48,1536]{3,2,1,0:T(8,128)(2,1)}) custom-call(bf16[4,256,384]{2,1,0:T(8,128)(2,1)} %bitcast.288, bf16[4,4,2,32,1536]{4,3,2,1,0:T(8,128)(2,1)} %bitcast.235, bf16[4,4,32,1536]{3,2,1,0:T(8,128)(2,1)} %get-tuple-element.151.refs_2_, ...), custom_call_target="tpu_custom_call" | custom-call | tf_op jit(solution)/shard_map/pallas_call | solution.py:95
  501.8 40.8 %shard_map.224 = (bf16[4,2,64,1536]{3,2,1,0:T(8,128)(2,1)}, bf16[4,48,2048]{2,1,0:T(8,128)(2,1)}) custom-call(bf16[2,4,64,1536]{3,2,1,0:T(8,128)(2,1)} %bitcast.279, bf16[4,4,2,48,2048]{4,3,2,1,0:T(8,128)(2,1)} %bitcast.227, bf16[4,4,48,2048]{3,2,1,0:T(8,128)(2,1)} %get-tuple-element.154.refs_2_), custom_call_target="tpu_custom_call" | custom-call | tf_op jit(solution)/shard_map/pallas_call | solution.py:95
  546.1 31.3 %shard_map.225 = (bf16[2,4,64,1536]{3,2,1,0:T(8,128)(2,1)}, bf16[4,48,1536]{2,1,0:T(8,128)(2,1)}, bf16[4,4,48,768]{3,2,1,0:T(8,128)(2,1)}) custom-call(bf16[2,64,1536]{2,1,0:T(8,128)(2,1)} %bitcast.264, bf16[4,4,2,48,1536]{4,3,2,1,0:T(8,128)(2,1)} %bitcast.215, bf16[4,4,48,1536]{3,2,1,0:T(8,128)(2,1)} %get-tuple-element.157.refs_2_, ...), custom_call_target="tpu_custom_call" | custom-call | tf_op jit(solution)/shard_map/pallas_call | solution.py:95
  582.1 8.1 convolution_convert_fusion.9
  590.2 26.9 %shard_map.226 = (bf16[4,2,64,1536]{3,2,1,0:T(8,128)(2,1)}, bf16[4,48,768]{2,1,0:T(8,128)(2,1)}, bf16[4,32,1536]{2,1,0:T(8,128)(2,1)}) custom-call(bf16[2,4,64,1536]{3,2,1,0:T(8,128)(2,1)} %bitcast.278, bf16[4,4,2,48,768]{4,3,2,1,0:T(8,128)(2,1)} %bitcast.243, bf16[4,4,48,768]{3,2,1,0:T(8,128)(2,1)} %get-tuple-element.159.refs_2_, ...), custom_call_target="tpu_custom_call" | custom-call | tf_op jit(solution)/shard_map/pallas_call | solution.py:95
  635.9 31.6 %shard_map.227 = (bf16[4,4,64,192]{3,2,1,0:T(8,128)(2,1)}, bf16[4,4,32,1536]{3,2,1,0:T(8,128)(2,1)}, bf16[4,4,48,2048]{3,2,1,0:T(8,128)(2,1)}, bf16[4,48,2048]{2,1,0:T(8,128)(2,1)}, bf16[4,48,1536]{2,1,0:T(8,128)(2,1)}) custom-call(bf16[4,2,2,64,192]{4,3,2,1,0:T(8,128)(2,1)} %bitcast.256, bf16[4,4,2,32,1536]{4,3,2,1,0:T(8,128)(2,1)} %bitcast.236, ...), custom_call_target="tpu_custom_call" | custom-call | tf_op jit(solution)/shard_map/pallas_call | solution.py:95
  667.5 9.4 %shard_map.228 = bf16[1024,384]{1,0:T(8,128)(2,1)} custom-call(bf16[1024,384]{1,0:T(8,128)(2,1)} %bitcast.290, bf16[1024,192]{1,0:T(8,128)(2,1)} %bitcast.324, f32[2,1024]{1,0:T(2,128)} %get-tuple-element.165.lse_ref, f32[1024,384]{1,0:T(8,128)} %concatenate.58.cos_ref, f32[1024,384]{1,0:T(8,128)} %concatenate.60.sin_ref), custom_call_target="tpu_custom_call" | custom-call | flops 3000000000 | bytes 1000000 | tf_op jit(solution)/shard_map/pallas_call | solution.py:652
  676.9 24.6 %shard_map.229 = (bf16[4,256,384]{2,1,0:T(8,128)(2,1)}, bf16[4,32,1536]{2,1,0:T(8,128)(2,1)}, bf16[4,4,48,1536]{3,2,1,0:T(8,128)(2,1)}) custom-call(bf16[4,256,384]{2,1,0:T(8,128)(2,1)} %bitcast.287, bf16[4,4,2,32,1536]{4,3,2,1,0:T(8,128)(2,1)} %bitcast.237, bf16[4,4,32,1536]{3,2,1,0:T(8,128)(2,1)} %get-tuple-element.166.refs_2_, ...), custom_call_target="tpu_custom_call" | custom-call | tf_op jit(solution)/shard_map/pallas_call | solution.py:95
  709.6 41.0 %shard_map.230 = (bf16[4,2,64,1536]{3,2,1,0:T(8,128)(2,1)}, bf16[4,48,2048]{2,1,0:T(8,128)(2,1)}, bf16[4,4,48,768]{3,2,1,0:T(8,128)(2,1)}) custom-call(bf16[2,4,64,1536]{3,2,1,0:T(8,128)(2,1)} %bitcast.266, bf16[4,4,2,48,2048]{4,3,2,1,0:T(8,128)(2,1)} %bitcast.229, bf16[4,4,48,2048]{3,2,1,0:T(8,128)(2,1)} %get-tuple-element.169.refs_2_, ...), custom_call_target="tpu_custom_call" | custom-call | tf_op jit(solution)/shard_map/pallas_call | solution.py:95
  754.3 50.0 %shard_map.231 = (bf16[4,48,768]{2,1,0:T(8,128)(2,1)}, bf16[4,48,1536]{2,1,0:T(8,128)(2,1)}, bf16[4,32,1536]{2,1,0:T(8,128)(2,1)}, bf16[4,48,2048]{2,1,0:T(8,128...) custom-call(bf16[4,4,2,48,768]{4,3,2,1,0:T(8,128)(2,1)} %bitcast.241, ...), custom_call_target="tpu_custom_call" | custom-call | tf_op jit(solution)/shard_map/pallas_call | solution.py:95
  810.7 5.6 fusion.26
  828.3 6.2 fusion.27
  855.6 20.4 %shard_map.232 = (bf16[4,48,768]{2,1,0:T(8,128)(2,1)}, bf16[4,48,1536]{2,1,0:T(8,128)(2,1)}) custom-call(bf16[4,48,768]{2,1,0:T(8,128)(2,1)} %get-tuple-element.177.refs_0_, bf16[4,48,1536]{2,1,0:T(8,128)(2,1)} %get-tuple-element.178.refs_1_), custom_call_target="tpu_custom_call" | custom-call | tf_op jit(solution)/shard_map/pallas_call | solution.py:95
  (317 shorter events, 198.2 us)
Async XLA Ops:
  0.6 4.3 copy-start.26
  7.2 3.9 copy-start.54
  106.3 195.0 %copy-start.34 = (f32[1,32,48]{2,1,0:T(8,128)}, f32[1,32,48]{2,1,0:T(8,128)S(1)}, u32[]{:S(2)}) copy-start(f32[1,32,48]{2,1,0:T(8,128)S(1)} %get-tuple-element.241) | copy-start | bytes 18436
  110.8 4.4 copy-start.40
  110.9 4.3 copy-start.48
  133.5 19.5 %copy-start.7 = (bf16[2,64,1536]{2,1,0:T(8,128)(2,1)S(1)}, bf16[2,64,1536]{2,1,0:T(8,128)(2,1)}, u32[]{:S(2)}) copy-start(bf16[2,64,1536]{2,1,0:T(8,128)(2,1)} %refs_0_.2) | copy-start | bytes 1179652
  193.2 4.6 copy-start.23
  235.9 27.2 %copy-start.1 = (f32[128,1536]{1,0:T(8,128)}, f32[128,1536]{1,0:T(8,128)S(1)}, u32[]{:S(2)}) copy-start(f32[128,1536]{1,0:T(8,128)S(1)} %get-tuple-element.209.hidden_ref) | copy-start | bytes 2359300
  235.9 27.2 %copy-start.46 = (f32[128]{0:T(128)}, f32[128]{0:T(128)S(1)}, u32[]{:S(2)}) copy-start(f32[128]{0:T(128)S(1)} %add_rsqrt_fusion.2) | copy-start | bytes 1540
  236.0 27.1 %copy-start.36 = (f32[1536]{0:T(1024)}, f32[1536]{0:T(1024)S(1)}, u32[]{:S(2)}) copy-start(f32[1536]{0:T(1024)S(1)} %mul.328) | copy-start | bytes 18436
  282.3 45.9 %slice-start.2 = ((s8[6291456]{0:T(1024)(128)(4,1)}), s8[2097152]{0:T(1024)(128)(4,1)S(1)}, s32[]{:S(2)}) async-start(s8[6291456]{0:T(1024)(128)(4,1)} %bitcast.218), calls=%async_computation.2 | async-start | bytes 4194304
  301.9 26.3 %slice-start.3 = ((s8[6291456]{0:T(1024)(128)(4,1)}), s8[4194304]{0:T(1024)(128)(4,1)S(1)}, s32[]{:S(2)}) async-start(s8[6291456]{0:T(1024)(128)(4,1)} %bitcast.218), calls=%async_computation.3 | async-start | bytes 8388608
  355.6 7.6 copy-start
  393.2 20.6 %copy-start.39 = (f32[128,1]{1,0:T(8,128)S(1)}, f32[128,1]{1,0:T(8,128)}, u32[]{:S(2)}) copy-start(f32[128,1]{1,0:T(8,128)} %get-tuple-element.148) | copy-start | bytes 1540
  393.2 20.7 %copy-start.35 = (f32[1,32,48]{2,1,0:T(8,128)S(1)}, f32[1,32,48]{2,1,0:T(8,128)}, u32[]{:S(2)}) copy-start(f32[1,32,48]{2,1,0:T(8,128)} %copy-done.34) | copy-start | bytes 18436
  393.2 20.8 %copy-start.15 = (f32[128,1536]{1,0:T(8,128)S(1)}, f32[128,1536]{1,0:T(8,128)}, u32[]{:S(2)}) copy-start(f32[128,1536]{1,0:T(8,128)} %get-tuple-element.144) | copy-start | bytes 2359300
  417.4 3.8 copy-start.62
  417.4 3.8 copy-start.64
  417.4 9.4 %slice-start = ((s8[4718592]{0:T(1024)(128)(4,1)}), s8[4194304]{0:T(1024)(128)(4,1)S(1)}, s32[]{:S(2)}) async-start(s8[4718592]{0:T(1024)(128)(4,1)} %bitcast.211), calls=%async_computation | async-start | bytes 8388608
  421.2 5.6 slice-start.1
  435.0 13.7 %copy-start.41 = (s32[4,4,2,64]{3,2,1,0:T(2,128)S(1)}, s32[4,4,2,64]{3,2,1,0:T(2,128)}, u32[]{:S(2)}) copy-start(s32[4,4,2,64]{3,2,1,0:T(2,128)} %copy-done.40) | copy-start | bytes 24580
  435.0 13.8 %copy-start.49 = (f32[48]{0:T(128)S(1)}, f32[48]{0:T(128)}, u32[]{:S(2)}) copy-start(f32[48]{0:T(128)} %copy-done.48) | copy-start | bytes 580
  546.1 31.3 %copy-start.14 = (f32[512,2048]{1,0:T(8,128)S(1)}, f32[512,2048]{1,0:T(8,128)}, u32[]{:S(2)}) copy-start(f32[512,2048]{1,0:T(8,128)} %copy-done.13) | copy-start | bytes 12582916
  582.1 8.1 copy-start.57
  582.1 8.1 copy-start.59
  619.7 13.3 %copy-start.5 = (f32[128,1536]{1,0:T(8,128)}, f32[128,1536]{1,0:T(8,128)S(1)}, u32[]{:S(2)}) copy-start(f32[128,1536]{1,0:T(8,128)S(1)} %multiply_add_fusion) | copy-start | bytes 2359300
  620.1 12.9 %slice-start.4 = ((s8[4718592]{0:T(1024)(128)(4,1)}), s8[4194304]{0:T(1024)(128)(4,1)S(1)}, s32[]{:S(2)}) async-start(s8[4718592]{0:T(1024)(128)(4,1)} %bitcast.231), calls=%async_computation.4 | async-start | bytes 8388608
  624.0 5.6 copy-start.24
  624.0 5.6 copy-start.53
  624.0 9.0 %slice-start.5 = ((s8[4718592]{0:T(1024)(128)(4,1)}), s8[524288]{0:T(1024)(128)(4,1)S(1)}, s32[]{:S(2)}) async-start(s8[4718592]{0:T(1024)(128)(4,1)} %bitcast.231), calls=%async_computation.5 | async-start | bytes 1048576
  754.3 50.0 %copy-start.28 = (bf16[4,32,1536]{2,1,0:T(8,128)(2,1)S(1)}, bf16[4,32,1536]{2,1,0:T(8,128)(2,1)}, u32[]{:S(2)}) copy-start(bf16[4,32,1536]{2,1,0:T(8,128)(2,1)} %get-tuple-element.186) | copy-start | bytes 1179652
  853.2 24.0 %copy-start.27 = (bf16[4,48,1536]{2,1,0:T(8,128)(2,1)S(1)}, bf16[4,48,1536]{2,1,0:T(8,128)(2,1)}, u32[]{:S(2)}) copy-start(bf16[4,48,1536]{2,1,0:T(8,128)(2,1)} %get-tuple-element.182) | copy-start | bytes 1769476
  (39 other events, 100.4 us)

commit v2 on v1

v2 whole, which is shorter than its diff:
```python
import functools

import jax
import jax.numpy as jnp
from jax import lax
from jax.experimental import pallas as pl
from jax.experimental.pallas import tpu as pltpu
from jax.sharding import PartitionSpec as P

HEAD = 96
LAYERS = 2
D = 1536
EPS = 1e-05
BASE = 100000.0
NEG = -1e30
F32 = jnp.float32
BF = jnp.bfloat16
MESH = pl.DeviceIdType.MESH
VMEM_LIMIT = 56 * 1024 * 1024


def place():
    dp, ctx, head = lax.axis_index("dp"), lax.axis_index("ctx"), lax.axis_index("head")
    y, zlo = lax.div(dp, 2), lax.rem(dp, 2)
    zhi, core = lax.div(ctx, 2), lax.rem(ctx, 2)
    return dict(dp=dp, ctx=ctx, x=head, y=y, zlo=zlo, zhi=zhi, core=core, z=zhi * 2 + zlo)


def dev(p, dx=0, dy=0, dz=0, dc=0):
    x = lax.rem(p["x"] + dx, 4)
    y = lax.rem(p["y"] + dy, 4)
    z = lax.rem(p["z"] + dz, 4)
    core = lax.rem(p["core"] + dc, 2)
    return (y * 2 + lax.rem(z, 2), lax.div(z, 2) * 2 + core, x)


def z_slot(z):
    return lax.rem(z, 2) * 2 + lax.div(z, 2)


class Op:
    def __init__(self, ins, outs, scratch, offsets, run, alias=()):
        self.ins, self.outs, self.scratch = list(ins), list(outs), list(scratch)
        self.offsets, self.run, self.alias = offsets, run, dict(alias)


class From:
    def __init__(self, op, k=0):
        self.op, self.k = op, k
        self.shape, self.dtype = op.outs[k]


def sems(n):
    return pltpu.SemaphoreType.DMA((n,))


def build(cid, ops):
    ins = [a for op in ops for a in op.ins if not isinstance(a, From)]
    outs = [o for op in ops for o in op.outs]
    scratch = [s for op in ops for s in op.scratch]
    offsets, alias, i0, o0 = [], {}, 0, 0
    for op in ops:
        for o in op.offsets:
            key = tuple(o.get(k, 0) for k in ("dx", "dy", "dz", "dc"))
            if key not in offsets:
                offsets.append(key)
        for i, o in op.alias.items():
            alias[i0 + i] = o0 + o
        i0 += sum(not isinstance(a, From) for a in op.ins)
        o0 += len(op.outs)
    n_in, n_out = len(ins), len(outs)

    def kernel(*refs):
        p = place()
        if offsets:
            barrier = pltpu.get_barrier_semaphore()
            for o in offsets:
                pl.semaphore_signal(barrier, inc=1, device_id=dev(p, *o), device_id_type=MESH)
            pl.semaphore_wait(barrier, len(offsets))
        i, o, s = 0, n_in, n_in + n_out
        runs, results = [], {}
        for op in ops:
            own = []
            for a in op.ins:
                if isinstance(a, From):
                    own.append(results[id(a.op)][a.k])
                else:
                    own.append(refs[i])
                    i += 1
            results[id(op)] = refs[o : o + len(op.outs)]
            runs.append(op.run(p, own, results[id(op)], refs[s : s + len(op.scratch)]))
            o, s = o + len(op.outs), s + len(op.scratch)
        while runs:
            live = []
            for r in runs:
                try:
                    next(r)
                    live.append(r)
                except StopIteration:
                    pass
            runs = live

    results = pl.pallas_call(
        kernel,
        out_shape=[jax.ShapeDtypeStruct(s, d) for s, d in outs],
        in_specs=[pl.BlockSpec(memory_space=pl.ANY)] * n_in,
        out_specs=[pl.BlockSpec(memory_space=pl.ANY)] * n_out,
        scratch_shapes=scratch,
        input_output_aliases=alias,
        compiler_params=pltpu.CompilerParams(
            collective_id=cid, has_side_effects=True, vmem_limit_bytes=VMEM_LIMIT
        ),
    )(*ins)
    split = []
    for op in ops:
        split.append(list(results[: len(op.outs)]))
        results = results[len(op.outs) :]
    return split


def idle(n):
    for _ in range(n):
        yield


def timed(op, *rounds):
    def run(*refs):
        steps = op.run(*refs)
        now = 0
        for r in rounds:
            yield from idle(r - now)
            now = r
            try:
                next(steps)
            except StopIteration:
                return
        yield
        for _ in steps:
            yield

    return Op(op.ins, op.outs, op.scratch, op.offsets, run, op.alias)


def chain(*ops):
    def run(p, ins, outs, scratch):
        for n, op in enumerate(ops):
            yield from op.run(p, ins if n == 0 else outs, outs, scratch[: len(op.scratch)])
            scratch = scratch[len(op.scratch) :]

    first = ops[0]
    return Op(
        first.ins,
        first.outs,
        [c for op in ops for c in op.scratch],
        [f for op in ops for f in op.offsets],
        run,
        first.alias,
    )


def send(src, dst, send_sem, recv_sem, target):
    c = pltpu.make_async_remote_copy(
        src_ref=src,
        dst_ref=dst,
        send_sem=send_sem,
        recv_sem=recv_sem,
        device_id=target,
        device_id_type=MESH,
    )
    c.start()
    return c


def copy(src, dst, sem):
    c = pltpu.make_async_copy(src, dst, sem)
    c.start()
    return c


X_OFF = [dict(dx=d) for d in (1, 3, 2)]
Y_OFF = [dict(dy=d) for d in (1, 3, 2)]
Z_OFF = [dict(dz=d) for d in (1, 3, 2)]
CORE_OFF = [dict(dc=1)]
CTX_OFF = [dict(dz=2, dc=0), dict(dz=2, dc=1), dict(dz=0, dc=1)]
SEQ_OFF = [
    dict(dx=dx, dz=dz, dc=dc) for dx in range(4) for dz in (0, 2) for dc in (0, 1)
][1:]
SHARD_OFF = [
    dict(dy=dy, dz=dz, dc=dc) for dy in range(4) for dz in range(4) for dc in (0, 1)
][1:]


def swap_op(a, out, offsets, near, far):
    block = jax.eval_shape(
        lambda v: near(dict(ctx=0, x=0, core=0, zhi=0), _Shape(v), _Shape(v))[0].value, a
    )
    n = len(offsets)

    def run(p, ins, outs, scratch):
        hold, s, r, k = scratch
        own, spot = near(p, ins[0], outs[0])
        inward = copy(own, hold, k.at[0])
        copies = []
        for i, o in enumerate(offsets):
            t = dev(p, **o)
            src, dst = far(p, ins[0], outs[0], t)
            copies.append(send(src, dst, s.at[i], r.at[i], t))
        inward.wait()
        outward = copy(hold, spot, k.at[1])
        yield
        outward.wait()
        for c in copies:
            c.wait()

    return Op(
        [a], [out], [pltpu.VMEM(block.shape, block.dtype), sems(n), sems(n), sems(2)], offsets, run
    )


class _Shape:
    def __init__(self, value):
        self.value = value

    @property
    def at(self):
        return self

    def __getitem__(self, index):
        return _Shape(self.value[index])


def gather_x(a):
    out = ((2, 4) + a.shape[1:], a.dtype)

    def near(p, i, o):
        return i, (o.at[:, p["x"]] if not isinstance(o, _Shape) else None)

    return swap_op(a, out, X_OFF, near, lambda p, i, o, t: (i, o.at[:, p["x"]]))


def scatter_x(a):
    out = ((4, 2) + a.shape[2:], a.dtype)
    return swap_op(
        a,
        out,
        X_OFF,
        lambda p, i, o: (i.at[:, p["x"]], o.at[p["x"]]),
        lambda p, i, o, t: (i.at[:, t[2]], o.at[p["x"]]),
    )


def swap_ctx(a):
    return swap_op(
        a,
        (a.shape, a.dtype),
        CTX_OFF,
        lambda p, i, o: (i.at[p["ctx"]], o.at[p["ctx"]]),
        lambda p, i, o, t: (i.at[t[1]], o.at[p["ctx"]]),
    )


def heads_to_tokens(a):
    return swap_op(
        a,
        ((4, 2, 2) + a.shape[2:], a.dtype),
        SEQ_OFF,
        lambda p, i, o: (
            i.at[p["ctx"], p["x"]],
            None if isinstance(o, _Shape) else o.at[p["x"], p["core"], p["zhi"]],
        ),
        lambda p, i, o, t: (i.at[t[1], t[2]], o.at[p["x"], p["core"], p["zhi"]]),
    )


def tokens_to_heads(a):
    return swap_op(
        a,
        ((4, 4) + a.shape[3:], a.dtype),
        SEQ_OFF,
        lambda p, i, o: (
            i.at[p["x"], p["core"], p["zhi"]],
            None if isinstance(o, _Shape) else o.at[p["ctx"], p["x"]],
        ),
        lambda p, i, o, t: (
            i.at[t[2], lax.rem(t[1], 2), lax.div(t[1], 2)],
            o.at[p["ctx"], p["x"]],
        ),
    )


def rows_x(a):
    return swap_op(
        a,
        ((4,) + a.shape, a.dtype),
        X_OFF,
        lambda p, i, o: (i, None if isinstance(o, _Shape) else o.at[p["x"]]),
        lambda p, i, o, t: (i, o.at[p["x"]]),
    )


def all_shards(a):
    return swap_op(
        a,
        ((8, 4) + a.shape, a.dtype),
        SHARD_OFF,
        lambda p, i, o: (i, None if isinstance(o, _Shape) else o.at[p["dp"], p["ctx"]]),
        lambda p, i, o, t: (i, o.at[p["dp"], p["ctx"]]),
    )


def line_off(axis, which=(1, 3, 2)):
    return [{"d" + axis: d} for d in which]


def ag_first(shard, order):
    whole = ((4, 4, 2) + shard.shape, shard.dtype)

    def run(p, ins, outs, scratch):
        hold, s, r, k = scratch
        dst = outs[0].at[p["y"], z_slot(p["z"]), p["core"]]
        inward = copy(ins[0], hold, k.at[0])
        copies = [
            send(ins[0], dst, s.at[i], r.at[i], dev(p, **o))
            for i, o in enumerate(line_off(order[0]))
        ]
        inward.wait()
        outward = copy(hold, dst, k.at[1])
        yield
        outward.wait()
        for c in copies:
            c.wait()

    return Op(
        [shard],
        [whole],
        [pltpu.VMEM(shard.shape, shard.dtype), sems(3), sems(3), sems(2)],
        line_off(order[0]),
        run,
    )


def ag_second(whole, order, which=(1, 3, 2)):
    def run(p, ins, outs, scratch):
        s, r = scratch
        if order == "zy":
            block = outs[0].at[p["y"], :, p["core"]]
        else:
            block = outs[0].at[:, z_slot(p["z"]), p["core"]]
        copies = [
            send(block, block, s.at[i], r.at[i], dev(p, **o))
            for i, o in enumerate(line_off(order[1], which))
        ]
        yield
        for c in copies:
            c.wait()

    n = len(which)
    return Op(
        [whole],
        [(whole.shape, whole.dtype)],
        [sems(n), sems(n)],
        line_off(order[1], which),
        run,
        {0: 0},
    )


def ag_third(whole):
    def run(p, ins, outs, scratch):
        s, r = scratch
        block = outs[0].at[:, :, p["core"]]
        c = send(block, block, s.at[0], r.at[0], dev(p, dc=1))
        yield
        c.wait()

    return Op([whole], [(whole.shape, whole.dtype)], [sems(1), sems(1)], CORE_OFF, run, {0: 0})


def ag_all(shard, order):
    first = ag_first(shard, order)
    whole = jax.ShapeDtypeStruct(*first.outs[0])
    return chain(first, ag_second(whole, order), ag_third(whole))


def _whole(shard):
    return jax.ShapeDtypeStruct((4, 4, 2) + shard.shape, shard.dtype)


def ag_rest(whole, order):
    return chain(ag_second(whole, order), ag_third(whole))


def add_into(dst, terms, rows):
    def body(k, carry):
        at = pl.ds(pl.multiple_of(k * 16, 16), 16)
        for n in range(dst.shape[0]):
            total = terms[0][n, at].astype(F32)
            for t in terms[1:]:
                total = total + t[n, at].astype(F32)
            dst[n, at] = total.astype(BF)
        return carry

    lax.fori_loop(0, rows // 16, body, 0)


def along(p, axis, d):
    return lax.rem(p["y"] + d, 4) if axis == "y" else z_slot(lax.rem(p["z"] + d, 4))


def rs_line(g, crossed, order):
    rows, cols = g.shape[2:]
    chunk = (4, rows, cols)

    def run(p, ins, outs, scratch):
        mine, other, got, load, s, r, k = scratch
        loads = []
        for d in (1, 3, 2, 0):
            at = along(p, order[0], d)
            if order[0] == "y":
                a, b = ins[0].at[at], ins[1].at[at]
            else:
                a, b = ins[0].at[:, at], ins[1].at[:, at]
            loads.append(
                (d, copy(a, mine.at[d], load.at[d]), copy(b, other.at[d], load.at[4 + d]))
            )
        copies = []
        for d, a, b in loads:
            a.wait()
            b.wait()
            add_into(mine.at[d], [mine.at[d], other.at[d]], rows)
            if d:
                copies.append(
                    send(
                        mine.at[d],
                        got.at[d - 1],
                        s.at[d - 1],
                        r.at[d - 1],
                        dev(p, **{"d" + order[0]: d}),
                    )
                )
        yield
        for c in copies:
            c.wait()
        add_into(other.at[0], [mine.at[0], got.at[0], got.at[1], got.at[2]], rows)
        out = copy(other.at[0], outs[0], k.at[0])
        yield
        out.wait()

    return Op(
        [g, crossed],
        [(chunk, BF)],
        [
            pltpu.VMEM((4,) + chunk, BF),
            pltpu.VMEM((4,) + chunk, BF),
            pltpu.VMEM((3,) + chunk, BF),
            sems(8),
            sems(3),
            sems(3),
            sems(1),
        ],
        line_off(order[0]),
        run,
    )


def rs_second(part, order):
    rows, cols = part.shape[1:]
    one = (1, rows, cols)

    def run(p, ins, outs, scratch):
        own, got, total, k, s, r = scratch
        load = copy(ins[0].at[pl.ds(along(p, order[1], 0), 1)], own, k.at[0])
        copies = []
        for i, o in enumerate(line_off(order[1])):
            d = o["d" + order[1]]
            copies.append(
                send(
                    ins[0].at[pl.ds(along(p, order[1], d), 1)],
                    got.at[i],
                    s.at[i],
                    r.at[i],
                    dev(p, **o),
                )
            )
        yield
        load.wait()
        for c in copies:
            c.wait()
        add_into(total, [own, got.at[0], got.at[1], got.at[2]], rows)
        out = copy(total, outs[0], k.at[1])
        yield
        out.wait()

    return Op(
        [part],
        [(one, BF)],
        [
            pltpu.VMEM(one, BF),
            pltpu.VMEM((3,) + one, BF),
            pltpu.VMEM(one, BF),
            sems(2),
            sems(3),
            sems(3),
        ],
        line_off(order[1]),
        run,
    )


def share_x(part):
    rows, cols = part.shape[1:]

    def run(p, ins, outs, scratch):
        hold, k, s, r = scratch
        inward = copy(ins[0], hold, k.at[0])
        dst = outs[0].at[pl.ds(p["x"], 1)]
        copies = [send(ins[0], dst, s.at[i], r.at[i], dev(p, **o)) for i, o in enumerate(X_OFF)]
        inward.wait()
        near = copy(hold, dst, k.at[1])
        yield
        near.wait()
        for c in copies:
            c.wait()

    return Op(
        [part],
        [((4, rows, cols), BF)],
        [pltpu.VMEM(part.shape, BF), sems(2), sems(3), sems(3)],
        X_OFF,
        run,
    )


def series(*ops):
    def run(p, ins, outs, scratch):
        for n, op in enumerate(ops):
            here, outs = outs[: len(op.outs)], outs[len(op.outs) :]
            yield from op.run(p, ins, here, scratch[: len(op.scratch)])
            scratch = scratch[len(op.scratch) :]
            ins = here

    return Op(
        ops[0].ins,
        [o for op in ops for o in op.outs],
        [c for op in ops for c in op.scratch],
        [f for op in ops for f in op.offsets],
        run,
    )


def shaped(op):
    return jax.ShapeDtypeStruct(*op.outs[-1])


def rs_finish(part, order):
    second = rs_second(part, order)
    return series(second, share_x(shaped(second)))


def rs_whole(mine, crossed, order):
    line = rs_line(mine, crossed, order)
    second = rs_second(shaped(line), order)
    return series(line, second, share_x(shaped(second)))


def sum_all(a):
    shape = a.shape
    axes = ("dx", "dy", "dz")

    def run(p, ins, outs, scratch):
        acc, got, k, s, r = scratch
        copy(ins[0], acc.at[0], k.at[0]).wait()
        for n, axis in enumerate(axes):
            copies = [
                send(
                    acc.at[n],
                    got.at[3 * n + d - 1],
                    s.at[3 * n + d - 1],
                    r.at[3 * n + d - 1],
                    dev(p, **{axis: d}),
                )
                for d in (1, 2, 3)
            ]
            yield
            for c in copies:
                c.wait()
            acc[n + 1] = acc[n] + got[3 * n] + got[3 * n + 1] + got[3 * n + 2]
        c = send(acc.at[3], got.at[9], s.at[9], r.at[9], dev(p, dc=1))
        yield
        c.wait()
        acc[4] = acc[3] + got[9]
        copy(acc.at[4], outs[0], k.at[0]).wait()

    return Op(
        [a],
        [(shape, F32)],
        [pltpu.VMEM((5,) + shape, F32), pltpu.VMEM((10,) + shape, F32), sems(1), sems(10), sems(10)],
        X_OFF + Y_OFF + Z_OFF + CORE_OFF,
        run,
    )


def pick(a, index, axis):
    return lax.dynamic_index_in_dim(a, index, axis, keepdims=False)


def rotated(y, cosine, sine):
    lane = lax.broadcasted_iota(jnp.int32, y.shape, 1)
    low = lax.rem(lane, HEAD) < HEAD // 2
    width = y.shape[1]
    turned = jnp.where(low, pltpu.roll(y, width - HEAD // 2, 1), pltpu.roll(y, HEAD // 2, 1))
    return y * cosine + turned * sine


def contract(a, b, da, db):
    return lax.dot_general(a, b, (((da,), (db,)), ((), ())), preferred_element_type=F32)


SCALE = HEAD ** (-0.5)


def masked(st, i):
    width = st.shape[0]
    key = lax.broadcasted_iota(jnp.int32, (256, 256), 0)
    query = lax.broadcasted_iota(jnp.int32, (256, 256), 1)
    last = jnp.where(key <= query, st[width - 256 :], NEG)
    return last if width == 256 else jnp.concatenate([st[: width - 256], last], axis=0)


def attend(qkv, out, lse):
    for i in range(4):
        rows = pl.ds(i * 256, 256)
        k = jnp.concatenate([qkv[j, :, 2 * HEAD : 3 * HEAD] for j in range(i + 1)], axis=0)
        v = jnp.concatenate([qkv[j, :, 3 * HEAD : 4 * HEAD] for j in range(i + 1)], axis=0)
        outs = []
        for n in range(2):
            q = qkv[i, :, n * HEAD : (n + 1) * HEAD]
            st = masked(contract(k, q, 1, 1) * SCALE, i)
            top = jnp.max(st, axis=0, keepdims=True)
            e = jnp.exp(st - top)
            total = jnp.sum(e, axis=0, keepdims=True)
            ot = contract(v, e.astype(BF), 0, 0)
            outs.append(ot * (1.0 / total))
            lse[n : n + 1, rows] = top + jnp.log(total)
        out[i] = jnp.concatenate(outs, axis=0).T.astype(BF)


def attend_back(qkv, do, lse, out, dq, dk, dv):
    dk[...] = jnp.zeros_like(dk)
    dv[...] = jnp.zeros_like(dv)
    for i in range(4):
        rows = pl.ds(i * 256, 256)
        width = (i + 1) * 256
        k = jnp.concatenate([qkv[j, :, 2 * HEAD : 3 * HEAD] for j in range(i + 1)], axis=0)
        v = jnp.concatenate([qkv[j, :, 3 * HEAD : 4 * HEAD] for j in range(i + 1)], axis=0)
        for n in range(2):
            cols = slice(n * HEAD, (n + 1) * HEAD)
            q, go = qkv[i, :, cols], do[i, :, cols]
            st = masked(contract(k, q, 1, 1) * SCALE, i)
            pr = jnp.exp(st - lse[n : n + 1, rows])
            dpt = contract(v, go, 1, 1)
            delta = jnp.sum(pr * dpt, axis=0, keepdims=True)
            ds = (pr * (dpt - delta)).astype(BF)
            dq[cols, rows] = contract(k, ds, 0, 0)
            dk[:width] += jnp.dot(ds, q, preferred_element_type=F32)
            dv[:width] += jnp.dot(pr.astype(BF), go, preferred_element_type=F32)
    for i in range(4):
        rows = pl.ds(i * 256, 256)
        g = jnp.concatenate([dq[:, rows].T * SCALE, dk[rows] * SCALE, dv[rows]], axis=1)
        out[i] = g.astype(BF)


def sigmoid(v):
    return 1.0 / (1.0 + jnp.exp(-v))


def row_scale(h):
    return lax.rsqrt(jnp.mean(h * h, axis=-1, keepdims=True) + EPS)


def own_rows(x):
    return pl.ds(pl.multiple_of(x * 64, 64), 64)


def tables(tab):
    cosine, sine = tab[:, :48], tab[:, 48:96]
    one = jnp.ones((tab.shape[0], 96), F32)
    return (
        jnp.concatenate([cosine] * 6 + [one], axis=1),
        jnp.concatenate([-sine, sine] * 3 + [one * 0.0], axis=1),
    )


def gain_row(gains, k):
    return jnp.concatenate(
        [gains[d, c, k : k + 1, :48] for d in range(8) for c in range(4)], axis=1
    )


class Links:
    def __init__(self, p, s, r, k):
        self.p, self.s, self.r, self.k, self.n, self.m = p, s, r, k, 0, 0

    def to(self, src, dst, target):
        c = send(src, dst, self.s.at[self.n], self.r.at[self.n], target)
        self.n += 1
        return c

    def near(self, src, dst):
        c = copy(src, dst, self.k.at[self.m])
        self.m += 1
        return c


def wait(copies):
    for c in copies:
        c.wait()


def gather_halves(net, x, own, dst):
    halves = []
    for s in range(2):
        at = dst.at[pl.ds(pl.multiple_of(s * 256 + x * 64, 64), 64)]
        halves.append(
            [net.to(own.at[s], at, dev(net.p, **o)) for o in X_OFF] + [net.near(own.at[s], at)]
        )
    return halves


def scatter_half(net, s, part, terms):
    copies = []
    for i, o in enumerate(X_OFF):
        t = dev(net.p, **o)
        src = part.at[pl.ds(pl.multiple_of(s * 256 + t[2] * 64, 64), 64)]
        copies.append(net.to(src, terms.at[i, s], t))
    return copies


def summed(x, s, part, terms):
    own = part[pl.ds(pl.multiple_of(s * 256 + x * 64, 64), 64)].astype(F32)
    return own + terms[0, s].astype(F32) + terms[1, s].astype(F32) + terms[2, s].astype(F32)


def swap_units(net, un, qv):
    p = net.p
    copies = []
    for o in CTX_OFF:
        t = dev(p, **o)
        copies.append(net.to(un.at[t[1]], qv.at[p["ctx"]], t))
    qv[pl.ds(p["ctx"], 1)] = un[pl.ds(p["ctx"], 1)]
    return copies


def columns(whole, cols):
    w = whole[:, :, :, :, cols]
    return w.reshape(32 * w.shape[3], w.shape[4])


N_SEMS = 96
LINK_SCRATCH = [sems(N_SEMS), sems(N_SEMS), sems(N_SEMS)]


def forward_op(l, normed, w_qkv, tabs, wholes, hidden, gains):
    last = l == LAYERS - 1
    ins = [normed, w_qkv, tabs, hidden, gains] + list(wholes)
    outs = {
        "qv": ((4, 256, 384), BF),
        "lse": ((2, 1024), F32),
        "tok": ((128, D), BF),
        "res": ((128, D), F32),
        "x2": ((512, D), BF),
        "gu": ((512, 2048), F32),
        "ac": ((512, 1024), BF),
        "hid": ((2, 64, D), F32),
        "nxt": ((2, 64, D), BF),
    }
    outs["xg"] = ((512, D), BF)
    names = list(outs)
    scratch = {
        "xg": ((512, D), BF),
        "wq": (w_qkv.shape, BF),
        "tab": ((512, 128), F32),
        "cs": ((512, 384), F32),
        "sn": ((512, 384), F32),
        "un": ((4, 256, 384), BF),
        "qv": ((4, 256, 384), BF),
        "lse": ((2, 1024), F32),
        "mx": ((4, 256, 192), BF),
        "mr": ((8, 128, 192), BF),
        "tok": ((128, D), BF),
        "wo": (wholes[0].shape, BF),
        "hid": ((2, 64, D), F32),
        "res": ((128, D), F32),
        "n2": ((2, 64, D), BF),
        "x2": ((512, D), BF),
        "wgu": (wholes[2].shape, BF),
        "wd": (wholes[1].shape, BF),
        "gu": ((512, 2048), F32),
        "ac": ((512, 1024), BF),
        "pt": ((512, D), BF),
        "tm": ((3, 2, 64, D), BF),
        "gains": ((8, 4, 8, 128), F32),
        "nxt": ((2, 64, D), BF),
    }
    keys = list(scratch)

    def run(p, ins, out_refs, refs):
        v = dict(zip(keys, refs[: len(keys)]))
        net = Links(p, *refs[len(keys) :])
        o = dict(zip(names, out_refs))
        whole = ins[5:]
        x = p["x"]
        saves = []

        def save(key):
            saves.append(net.near(v[key], o[key]))

        if l:
            halves = gather_halves(net, x, ins[0], v["xg"])
        else:
            halves = [
                [
                    net.near(ins[0].at[s, k], v["xg"].at[pl.ds(s * 256 + k * 64, 64)])
                    for k in range(4)
                ]
                for s in range(2)
            ]
        early = [net.near(ins[1], v["wq"]), net.near(ins[4], v["gains"])]
        for s in range(2):
            for k in range(4):
                early.append(
                    net.near(
                        ins[2].at[k, pl.ds(64 * s, 64)],
                        v["tab"].at[pl.ds(s * 256 + k * 64, 64)],
                    )
                )
        late = [net.near(ins[3], v["hid"])]
        wait(early)
        cosine, sine = tables(v["tab"][...])
        v["cs"][...] = cosine
        v["sn"][...] = sine
        for s in range(2):
            wait(halves[s])
            rows = pl.ds(s * 256, 256)
            if not l:
                gain = gain_row(v["gains"], 0)
                for k in range(4):
                    part = pl.ds(s * 256 + k * 64, 64)
                    h = v["xg"][part].astype(F32)
                    v["xg"][part] = (h * row_scale(h) * gain).astype(BF)
            for u in range(2):
                y = jnp.dot(
                    v["xg"][rows], columns(v["wq"], slice(u * 384, u * 384 + 384)), preferred_element_type=F32
                )
                v["un"][s * 2 + u] = rotated(y, v["cs"][rows], v["sn"][rows]).astype(BF)
        moves = swap_units(net, v["un"], v["qv"])
        save("xg")
        yield
        wait(moves)
        save("qv")
        attend(v["qv"], v["mx"], v["lse"])
        save("lse")
        moves = []
        for off in SEQ_OFF:
            t = dev(p, **off)
            moves.append(
                net.to(
                    v["mx"].at[t[1], own_rows(t[2])],
                    v["mr"].at[p["x"] * 2 + p["core"], own_rows(p["zhi"])],
                    t,
                )
            )
        v["mr"][pl.ds(x * 2 + p["core"], 1), own_rows(p["zhi"])] = v["mx"][
            pl.ds(p["ctx"], 1), own_rows(x)
        ]
        yield
        load = net.near(whole[0], v["wo"])
        wait(moves)
        v["tok"][...] = jnp.concatenate([v["mr"][g] for g in range(8)], axis=1)
        save("tok")
        load.wait()
        wait(late)
        gain = gain_row(v["gains"], 2 + l)
        for s in range(2):
            rows = pl.ds(s * 64, 64)
            for c in range(3):
                cols = slice(c * 512, (c + 1) * 512)
                v["res"][rows, cols] = v["hid"][s, :, cols] + jnp.dot(
                    v["tok"][rows], columns(v["wo"], cols), preferred_element_type=F32
                )
            h = v["res"][rows]
            v["n2"][s] = (h * row_scale(h) * gain).astype(BF)
        halves = gather_halves(net, x, v["n2"], v["x2"])
        save("res")
        yield
        yield
        loads = [net.near(whole[2], v["wgu"]), net.near(whole[1], v["wd"])]
        wait(loads[:1])
        backs = []
        for s in range(2):
            wait(halves[s])
            rows = pl.ds(s * 256, 256)
            for j in range(2):
                cols, more = slice(j * 512, (j + 1) * 512), slice(1024 + j * 512, 1536 + j * 512)
                gate = jnp.dot(v["x2"][rows], columns(v["wgu"], cols), preferred_element_type=F32)
                up = jnp.dot(v["x2"][rows], columns(v["wgu"], more), preferred_element_type=F32)
                v["gu"][rows, cols] = gate
                v["gu"][rows, more] = up
                v["ac"][rows, cols] = (gate * sigmoid(gate) * up).astype(BF)
            if s == 0:
                wait(loads[1:])
            for c in range(3):
                cols = slice(c * 512, (c + 1) * 512)
                v["pt"][rows, cols] = jnp.dot(
                    v["ac"][rows], columns(v["wd"], cols), preferred_element_type=F32
                ).astype(BF)
            backs.append(scatter_half(net, s, v["pt"], v["tm"]))
            yield
        save("x2")
        save("gu")
        save("ac")
        gain = gain_row(v["gains"], 1)
        for s in range(2):
            wait(backs[s])
            h = v["res"][pl.ds(s * 64, 64)] + summed(x, s, v["pt"], v["tm"])
            v["hid"][s] = h
            if last:
                v["nxt"][s] = h.astype(BF)
            else:
                v["nxt"][s] = (h * row_scale(h) * gain).astype(BF)
        save("hid")
        save("nxt")
        yield
        wait(saves)

    return names, Op(
        ins,
        list(outs.values()),
        [pltpu.VMEM(*scratch[k]) for k in keys] + LINK_SCRATCH,
        X_OFF + CTX_OFF + SEQ_OFF,
        run,
    )


def norm_back_rows(h, gain, upstream):
    scale = row_scale(h)
    unit = h * scale
    weighted = upstream * gain
    back = scale * (weighted - unit * jnp.mean(weighted * unit, axis=-1, keepdims=True))
    return back, jnp.sum(upstream * unit, axis=0, keepdims=True)


def cross(net, g, mine, crossed):
    p = net.p
    return [
        net.to(g.at[:, 1 - p["core"]], crossed, dev(p, dc=1)),
        net.near(g.at[:, p["core"]], mine),
    ]


def mlp_back_op(l, grad_b, gradient, w_gu, w_down, w_out, gu, ac, x2, res, tok, gains):
    ins = [grad_b, gradient, w_gu, w_down, w_out, gu, ac, x2, res, tok, gains]
    outs = {
        "md": ((16, 32, D), BF),
        "cd": ((16, 32, D), BF),
        "mg": ((16, 48, 2048), BF),
        "cg": ((16, 48, 2048), BF),
        "mo": ((16, 48, D), BF),
        "co": ((16, 48, D), BF),
        "gr": ((128, D), F32),
        "gg": ((1, D), F32),
        "gm": ((8, 128, 192), BF),
    }
    names = list(outs)
    scratch = {
        "gb": ((512, D), BF),
        "gr": ((128, D), F32),
        "wgu": ((D, 2048), BF),
        "wd": ((1024, D), BF),
        "wo": ((D, D), BF),
        "gu": ((512, 2048), F32),
        "ac": ((512, 1024), BF),
        "x2": ((512, D), BF),
        "res": ((128, D), F32),
        "tok": ((128, D), BF),
        "gains": ((8, 4, 8, 128), F32),
        "dgu": ((512, 2048), BF),
        "pt": ((512, D), BF),
        "tm": ((3, 2, 64, D), BF),
        "gd": ((16, 2, 32, D), BF),
        "gg2": ((16, 2, 48, 2048), BF),
        "go": ((16, 2, 48, D), BF),
        "rb": ((128, D), BF),
        "gg": ((1, D), F32),
        "gm": ((8, 128, 192), BF),
    }
    keys = list(scratch)

    def run(p, ins, out_refs, refs):
        v = dict(zip(keys, refs[: len(keys)]))
        net = Links(p, *refs[len(keys) :])
        o = dict(zip(names, out_refs))
        x = p["x"]
        if l == LAYERS - 1:
            halves = [
                [net.near(ins[0].at[pl.ds(s * 256, 256)], v["gb"].at[pl.ds(s * 256, 256)])]
                for s in range(2)
            ]
        else:
            halves = gather_halves(net, x, ins[0], v["gb"])
        loads = [net.near(ins[3], v["wd"]), net.near(ins[5], v["gu"]), net.near(ins[2], v["wgu"])]
        more = [
            net.near(ins[6], v["ac"]),
            net.near(ins[7], v["x2"]),
            net.near(ins[8], v["res"]),
            net.near(ins[1], v["gr"]),
            net.near(ins[10], v["gains"]),
            net.near(ins[4], v["wo"]),
            net.near(ins[9], v["tok"]),
        ]
        yield
        wait(loads[:2])
        backs = []
        for s in range(2):
            wait(halves[s])
            rows = pl.ds(s * 256, 256)
            for j in range(2):
                cols, high = slice(j * 512, (j + 1) * 512), slice(1024 + j * 512, 1536 + j * 512)
                ga = contract(v["gb"][rows], v["wd"][cols], 1, 1)
                gate, up = v["gu"][rows, cols], v["gu"][rows, high]
                sg = sigmoid(gate)
                v["dgu"][rows, cols] = (ga * up * sg * (1.0 + gate * (1.0 - sg))).astype(BF)
                v["dgu"][rows, high] = (ga * gate * sg).astype(BF)
            if s == 0:
                wait(loads[2:])
            for c in range(3):
                cols = slice(c * 512, (c + 1) * 512)
                v["pt"][rows, cols] = contract(v["dgu"][rows], v["wgu"][cols], 1, 1).astype(BF)
            backs.append(scatter_half(net, s, v["pt"], v["tm"]))
            yield
        wait(more)
        for i in range(4):
            for c in range(3):
                cols = slice(c * 512, (c + 1) * 512)
                g = contract(v["ac"][:, i * 256 : (i + 1) * 256], v["gb"][:, cols], 0, 0)
                v["gd"][i * 4 : (i + 1) * 4, :, :, cols] = g.astype(BF).reshape(4, 2, 32, 512)
        ends = cross(net, v["gd"], o["md"], o["cd"])
        for i in range(4):
            for c in range(4):
                cols = slice(c * 512, (c + 1) * 512)
                g = contract(v["x2"][:, i * 384 : (i + 1) * 384], v["dgu"][:, cols], 0, 0)
                v["gg2"][i * 4 : (i + 1) * 4, :, :, cols] = g.astype(BF).reshape(4, 2, 48, 512)
        ends += cross(net, v["gg2"], o["mg"], o["cg"])
        yield
        total = jnp.zeros((1, D), F32)
        gain = gain_row(v["gains"], 2 + l)
        for s in range(2):
            wait(backs[s])
            rows = pl.ds(s * 64, 64)
            back, gain_grad = norm_back_rows(
                v["res"][rows], gain, summed(x, s, v["pt"], v["tm"])
            )
            total = total + gain_grad
            gr = v["gr"][rows] + back
            v["gr"][rows] = gr
            v["rb"][rows] = gr.astype(BF)
        v["gg"][...] = total
        ends += [net.near(v["gr"], o["gr"]), net.near(v["gg"], o["gg"])]
        for j in range(4):
            g = contract(v["rb"][...], v["wo"][j * 384 : (j + 1) * 384], 1, 1).astype(BF)
            v["gm"][2 * j] = g[:, :192]
            v["gm"][2 * j + 1] = g[:, 192:]
        ends += [net.near(v["gm"], o["gm"])]
        for i in range(4):
            for c in range(3):
                cols = slice(c * 512, (c + 1) * 512)
                g = contract(v["tok"][:, i * 384 : (i + 1) * 384], v["rb"][:, cols], 0, 0)
                v["go"][i * 4 : (i + 1) * 4, :, :, cols] = g.astype(BF).reshape(4, 2, 48, 512)
        ends += cross(net, v["go"], o["mo"], o["co"])
        yield
        wait(ends)

    return names, Op(
        ins,
        list(outs.values()),
        [pltpu.VMEM(*scratch[k]) for k in keys] + LINK_SCRATCH,
        X_OFF + CORE_OFF,
        run,
    )


def attend_back_op(l, gm, qv, lse, tabs, w_qkv, xg, hidden, gains, gr):
    ins = [gm, qv, lse, tabs, w_qkv, xg, hidden, gains, gr]
    outs = {
        "mq": ((16, 48, 768), BF),
        "cq": ((16, 48, 768), BF),
        "gr": ((2, 64, D), F32),
        "gb": ((2, 64, D), BF),
        "gg": ((1, D), F32),
    }
    names = list(outs)
    scratch = {
        "do": ((4, 256, 192), BF),
        "qv": ((4, 256, 384), BF),
        "lse": ((2, 1024), F32),
        "tab": ((512, 128), F32),
        "cs": ((512, 384), F32),
        "sn": ((512, 384), F32),
        "un": ((4, 256, 384), BF),
        "dqkv": ((4, 256, 384), BF),
        "dq": ((192, 1024), F32),
        "dk": ((1024, HEAD), F32),
        "dv": ((1024, HEAD), F32),
        "wq": ((D, 768), BF),
        "xg": ((512, D), BF),
        "hid": ((2, 64, D), F32),
        "gains": ((8, 4, 8, 128), F32),
        "gr": ((2, 64, D), F32),
        "gb": ((2, 64, D), BF),
        "gg": ((1, D), F32),
        "pt": ((512, D), BF),
        "tm": ((3, 2, 64, D), BF),
        "gq": ((16, 2, 48, 768), BF),
    }
    keys = list(scratch)

    def run(p, ins, out_refs, refs):
        v = dict(zip(keys, refs[: len(keys)]))
        net = Links(p, *refs[len(keys) :])
        o = dict(zip(names, out_refs))
        x = p["x"]
        dst = v["do"].at[p["ctx"], own_rows(x)]
        moves = []
        for off in SEQ_OFF:
            t = dev(p, **off)
            src = ins[0].at[t[2] * 2 + lax.rem(t[1], 2), own_rows(lax.div(t[1], 2))]
            moves.append(net.to(src, dst, t))
        moves.append(net.near(ins[0].at[x * 2 + p["core"], own_rows(p["zhi"])], dst))
        moves += [net.near(ins[1], v["qv"]), net.near(ins[2], v["lse"])]
        tabs = []
        for n in range(2):
            for k in range(4):
                tabs.append(
                    net.near(
                        ins[3].at[k, pl.ds(64 * n, 64)],
                        v["tab"].at[pl.ds(n * 256 + k * 64, 64)],
                    )
                )
        loads = [net.near(ins[4], v["wq"]), net.near(ins[5], v["xg"]), net.near(ins[6], v["hid"])]
        loads += [net.near(ins[7], v["gains"]), net.near(ins[8], v["gr"])]
        wait(tabs)
        cosine, sine = tables(v["tab"][...])
        v["cs"][...] = cosine
        v["sn"][...] = sine
        yield
        wait(moves)
        attend_back(v["qv"], v["do"], v["lse"], v["un"], v["dq"], v["dk"], v["dv"])
        moves = swap_units(net, v["un"], v["dqkv"])
        yield
        wait(loads)
        wait(moves)
        backs = []
        for s in range(2):
            rows = pl.ds(s * 256, 256)
            for u in range(2):
                g = v["dqkv"][2 * s + u].astype(F32)
                v["dqkv"][2 * s + u] = rotated(g, v["cs"][rows], -v["sn"][rows]).astype(BF)
            d = jnp.concatenate([v["dqkv"][2 * s], v["dqkv"][2 * s + 1]], axis=1)
            for c in range(3):
                cols = slice(c * 512, (c + 1) * 512)
                v["pt"][rows, cols] = contract(d, v["wq"][cols], 1, 1).astype(BF)
            backs.append(scatter_half(net, s, v["pt"], v["tm"]))
        yield
        for u in range(2):
            d = jnp.concatenate([v["dqkv"][u], v["dqkv"][2 + u]], axis=0)
            for i in range(4):
                g = contract(v["xg"][:, i * 384 : (i + 1) * 384], d, 0, 0)
                v["gq"][i * 4 : (i + 1) * 4, :, :, u * 384 : (u + 1) * 384] = g.astype(BF).reshape(
                    4, 2, 48, 384
                )
        ends = cross(net, v["gq"], o["mq"], o["cq"])
        yield
        total = jnp.zeros((1, D), F32)
        gain = gain_row(v["gains"], l)
        for s in range(2):
            wait(backs[s])
            back, gain_grad = norm_back_rows(v["hid"][s], gain, summed(x, s, v["pt"], v["tm"]))
            total = total + gain_grad
            gr = v["gr"][s] + back
            v["gr"][s] = gr
            v["gb"][s] = gr.astype(BF)
        v["gg"][...] = total
        ends += [net.near(v[k], o[k]) for k in ("gr", "gb", "gg")]
        yield
        wait(ends)

    return names, Op(
        ins,
        list(outs.values()),
        [pltpu.VMEM(*scratch[k]) for k in keys] + LINK_SCRATCH,
        X_OFF + CTX_OFF + SEQ_OFF,
        run,
    )


def rope_rows(positions):
    half = HEAD // 2
    frequency = BASE ** (-(jnp.arange(half, dtype=F32) * 2.0 / HEAD))
    angles = positions.astype(F32)[:, None] * frequency
    return jnp.concatenate([jnp.cos(angles), jnp.sin(angles), jnp.zeros((128, 32), F32)], axis=1)


def ff_quarter(a, x):
    rows = a.shape[0]
    return pick(a.reshape(rows, 32, 4, 32), x, 2).reshape(rows, 1024)


def pack_qkv(q, k, v, x):
    rows = q.shape[0]
    q = lax.dynamic_slice_in_dim(q, x * 384, 384, 1).reshape(rows, 2, 192)
    k = lax.dynamic_slice_in_dim(k, x * 192, 192, 1).reshape(rows, 2, 96)
    v = lax.dynamic_slice_in_dim(v, x * 192, 192, 1).reshape(rows, 2, 96)
    return jnp.concatenate([q, k, v], axis=2).reshape(rows, 768)


def unpack_kernel(*refs):
    ins, (q_ref, k_ref, v_ref, o_ref, gate_ref, up_ref, down_ref) = refs[:-7], refs[-7:]
    row = lax.broadcasted_iota(jnp.int32, (512, 512), 0)
    col = lax.broadcasted_iota(jnp.int32, (512, 512), 1)
    place_of = lax.rem(row, 128) // 32 * 128 + row // 128 * 32 + lax.rem(row, 32)
    turn = jnp.where(place_of == col, 1.0, 0.0).astype(BF)
    for l in range(LAYERS):
        qkv, out, down, gu = ins[4 * l : 4 * l + 4]
        q_ref[l] = jnp.concatenate(
            [qkv[x, :, u * 384 : u * 384 + 192] for x in range(4) for u in range(2)], axis=1
        ).astype(F32)
        k_ref[l] = jnp.concatenate(
            [qkv[x, :, u * 384 + 192 : u * 384 + 288] for x in range(4) for u in range(2)], axis=1
        ).astype(F32)
        v_ref[l] = jnp.concatenate(
            [qkv[x, :, u * 384 + 288 : u * 384 + 384] for x in range(4) for u in range(2)], axis=1
        ).astype(F32)
        o_ref[l] = (out[0].astype(F32) + out[1].astype(F32)) + (
            out[2].astype(F32) + out[3].astype(F32)
        )
        for x in range(4):
            down_ref[l, x * 32 : (x + 1) * 32] = down[x].astype(F32)
        for n, ref in enumerate((gate_ref, up_ref)):
            for t in range(8):
                at = n * 1024 + t * 128
                piece = jnp.concatenate([gu[x, :, at : at + 128] for x in range(4)], axis=1)
                ref[l, :, t * 512 : (t + 1) * 512] = jnp.dot(
                    piece, turn, preferred_element_type=F32
                )


def unpack(ends):
    sizes = [(48, D), (48, 768), (48, 768), (48, D), (48, 4096), (48, 4096), (128, D)]
    return pl.pallas_call(
        unpack_kernel,
        out_shape=[jax.ShapeDtypeStruct((LAYERS,) + z, F32) for z in sizes],
        compiler_params=pltpu.CompilerParams(vmem_limit_bytes=VMEM_LIMIT),
        cost_estimate=pl.CostEstimate(flops=10**9, bytes_accessed=10**7, transcendentals=0),
    )(*ends)


AG_ROUNDS = ((0, 1, 2, 3), (0, 1, 4, 5), (0, 2, 6, 7), (0, 2, 6, 7))
RS_QKV, RS_OUT, RS_DOWN, RS_GU = "yz", "zy", "yz", "yz"


def per_device(
    inputs,
    positions,
    cotangent,
    attn_gain,
    query_weight,
    key_matrix,
    value_matrix,
    out_weight,
    mlp_gain,
    gate_weight,
    up_weight,
    down_weight,
):
    p = place()
    x = p["x"]

    shards = []
    for l in range(LAYERS):
        gu = jnp.concatenate([ff_quarter(gate_weight[l], x), ff_quarter(up_weight[l], x)], axis=1)
        down = lax.dynamic_slice_in_dim(down_weight[l], x * 32, 32, 0)
        qkv = pack_qkv(query_weight[l], key_matrix[l], value_matrix[l], x)
        shards.append((qkv, out_weight[l], down, gu))
    orders = ("zy", "yz", "yz", "zy")

    gains = jnp.zeros((8, 128), F32)
    gains = gains.at[:2, :48].set(attn_gain.astype(F32)).at[2:4, :48].set(mlp_gain.astype(F32))
    hidden = inputs.astype(F32)
    saved = []
    whole = []
    tokens = timed(gather_x(inputs), 0, 3)
    tab = timed(rows_x(rope_rows(positions.reshape(128))), 0, 3)
    gain = timed(all_shards(gains), 0, 3)
    w = [timed(ag_all(a, o), *t) for a, o, t in zip(shards[0], orders, AG_ROUNDS)]
    names, fg = forward_op(
        0, From(tokens), From(w[0]), From(tab), [From(a) for a in w[1:]], hidden, From(gain)
    )
    nxt = [
        timed(ag_all(shards[1][0], orders[0]), 5, 6, 8, 9),
        timed(chain(ag_first(shards[1][1], orders[1]), ag_second(_whole(shards[1][1]), orders[1])), 5, 6, 9),
        timed(ag_first(shards[1][2], orders[2]), 5, 6),
        timed(ag_first(shards[1][3], orders[3]), 5, 6),
    ]
    done = build(1, w + [tokens, tab, gain, timed(fg, 3)] + nxt)
    whole.append([d[0] for d in done[:4]])
    tabs, gains_g = done[5][0], done[6][0]
    kept = dict(zip(names, done[7]))
    kept["hidden"] = hidden
    saved.append(kept)
    second = [d[0] for d in done[8:]]
    hidden = kept["hid"]
    w = [
        timed(ag_third(second[1]), 0, 1),
        timed(ag_rest(second[2], orders[2]), 0, 3, 4),
        timed(ag_rest(second[3], orders[3]), 0, 3, 4),
    ]
    names, fg = forward_op(
        1, kept["nxt"], second[0], tabs, [From(a) for a in w], hidden, gains_g
    )
    done = build(2, w + [fg, timed(gather_x(cotangent), 0, 4)])
    whole.append([second[0]] + [d[0] for d in done[:3]])
    kept = dict(zip(names, done[3]))
    kept["hidden"] = hidden
    saved.append(kept)
    output = kept["nxt"]
    cot_g = done[4][0]

    gradient = cotangent.astype(F32)
    grad_b = cot_g.reshape(512, D)
    ends = [[None] * 4 for _ in range(LAYERS)]
    gain_grads = [None] * 4
    by_line = lambda a: a.reshape((4, 4) + a.shape[1:])
    for l in reversed(range(LAYERS)):
        kept = saved[l]
        w_qkv, w_out, w_down, w_gu = whole[l]
        w_qkv, w_out = w_qkv.reshape(D, 768), w_out.reshape(D, D)
        w_down, w_gu = w_down.reshape(1024, D), w_gu.reshape(D, 2048)
        names, fg = mlp_back_op(
            l, grad_b, gradient.reshape(128, D), w_gu, w_down, w_out, kept["gu"], kept["ac"],
            kept["x2"], kept["res"], kept["tok"], gains_g,
        )
        if l == 1:
            (r,) = build(4, [fg])
        else:
            r, (part_out1,), (part_qkv1,), (one_gu,), (one_down,) = build(
                5,
                [
                    fg,
                    timed(rs_line(r["mo"], r["co"], RS_OUT), 0, 3, 4),
                    timed(rs_line(q["mq"], q["cq"], RS_QKV), 0, 3, 4),
                    timed(rs_second(part_gu, RS_GU), 0, 3, 4),
                    timed(rs_second(part_down, RS_DOWN), 0, 3, 4),
                ],
            )
        r = {k: by_line(a) if a.shape[0] == 16 else a for k, a in zip(names, r)}
        gain_grads[2 + l] = r["gg"]
        names, fg = attend_back_op(
            l, r["gm"], kept["qv"], kept["lse"], tabs, w_qkv, kept["xg"], kept["hidden"], gains_g,
            r["gr"].reshape(2, 64, D),
        )
        bg = [
            timed(rs_line(r["mg"], r["cg"], RS_GU), 0, 4, 5),
            timed(rs_line(r["md"], r["cd"], RS_DOWN), 0, 4, 5),
        ]
        if l == 0:
            bg.append(timed(rs_line(r["mo"], r["co"], RS_OUT), 1, 4, 5))
            bg += [share_x(one_gu), share_x(one_down)]
            bg += [rs_finish(part_out1, RS_OUT), rs_finish(part_qkv1, RS_QKV)]
        q, *rest = build(6 + (l == 0), [fg] + bg)
        part_gu, part_down = rest[0][0], rest[1][0]
        if l == 0:
            part_out = rest[2][0]
            ends[1] = [rest[6][-1], rest[5][-1], rest[4][-1], rest[3][-1]]
        q = {k: by_line(a) if a.shape[0] == 16 else a for k, a in zip(names, q)}
        gain_grads[l] = q["gg"]
        gradient, grad_b = q["gr"], q["gb"]

    sums = jnp.zeros((8, D), F32).at[:4].set(jnp.concatenate(gain_grads, axis=0))
    tail = build(
        8,
        [
            rs_whole(q["mq"], q["cq"], RS_QKV),
            rs_finish(part_gu, RS_GU),
            rs_finish(part_down, RS_DOWN),
            rs_finish(part_out, RS_OUT),
            sum_all(sums),
        ],
    )
    ends[0][0], ends[0][3], ends[0][2], ends[0][1], gain_sum = [t[-1] for t in tail]
    grads = unpack(ends[0] + ends[1])

    block = p["dp"] * 4 + p["ctx"]
    gain_own = pick(gain_sum[:4].reshape(4, 32, 48), block, 1)
    return (
        output,
        gradient.reshape(2, 64, D),
        gain_own[:2],
        grads[0],
        grads[1],
        grads[2],
        grads[3],
        gain_own[2:],
        grads[4],
        grads[5],
        grads[6],
    )


def solution(mesh):
    tokens = P("dp", ("ctx", "head"), None)
    vector = P(None, ("dp", "ctx"))
    matrix = P(None, ("dp", "ctx"), None)
    return jax.shard_map(
        per_device,
        mesh=mesh,
        in_specs=(
            tokens,
            P("dp", ("ctx", "head")),
            tokens,
            vector,
            matrix,
            matrix,
            matrix,
            matrix,
            vector,
            matrix,
            matrix,
            matrix,
        ),
        out_specs=(
            tokens,
            tokens,
            vector,
            matrix,
            matrix,
            matrix,
            matrix,
            vector,
            matrix,
            matrix,
            matrix,
        ),
        check_vma=False,
    )
```

time: 894 us -> 576 us (0.64)
  Pallas kernels: 667 us -> 551 us
  matrix products: 85.5 us -> 0 us
  local copies, waits for them, and re-layouts: 90.6 us -> 14.2 us
  other arithmetic: 42.6 us -> 6.02 us
    dot_general x20 -> x0, matrix products: 85.5 us -> none  [the longest x16 66.5 us: contract(): lax.dot_general(a, b, (((da,), (db,)), ((), ())), preferred_element_type=...]
    pallas_call x22 -> x7, Pallas kernels: 616 us -> 543 us  [build(): pl.pallas_call(kernel, out_shape=[jax.ShapeDtypeStruct(s, d) for s, d in...]
    pallas_call x8 -> x1, Pallas kernels: 50.9 us -> 7.99 us  [unpack(): pl.pallas_call(unpack_kernel, out_shape=[jax.ShapeDtypeStruct((LAYERS,) +...]
    slice x23 -> x0, local copies, waits for them, and re-layouts: 38.4 us -> none  [the longest x6 25.6 us: per_device(): a_gu[1]]
    reduce_sum x15 -> x0, other arithmetic: 16.7 us -> none  [the longest x4 7.06 us: per_device(): grad_normed = jnp.sum(terms.astype(F32), axis=0).reshape(128, D)]
    concatenate x8 -> x1, local copies, waits for them, and re-layouts: 13.4 us -> 0.07 us  [rope_rows(): jnp.concatenate([jnp.cos(angles), jnp.sin(angles), jnp.zeros((128, 32), F...]
    another operation x8 -> x0, other arithmetic: 11.2 us -> none  [the longest x7 10.5 us: per_device(): jnp.stack([reduced[l][k] for l in range(LAYERS)])]
    convert_element_type x8 -> x1, local copies, waits for them, and re-layouts: 10.3 us -> 0.08 us  [rope_rows(): angles = positions.astype(F32)[:, None] * frequency]
where the time goes in v2:
time: 576 us; the launch traced here: 572 us
  Pallas kernels  551 us (96%)
  local copies, waits for them, and re-layouts  14.2 us (2%)
  other arithmetic  6.02 us (1%)
    pallas_call x7, Pallas kernels, build(): pl.pallas_call(kernel, out_shape=[jax.ShapeDtypeStruct(s, d) for s, d in...  543 us

profile of v2, /device:TPU:0, one launch (start us, length us, event | category | flops | bytes accessed | tf_op | source)
XLA Modules:
  0.0 572.1 jit_solution(9094393828505916077)
XLA Ops:
  0.7 1.0 fusion.4
  1.8 0.9 fusion.5
  3.0 1.1 fusion.3
  4.3 0.6 copy.62
  5.4 0.6 copy.61
  6.1 0.5 copy.57
  6.7 0.5 copy.56
  7.5 0.7 pad_maximum_fusion.1.refs_11_
  8.2 0.5 copy.54
  8.6 0.5 copy.55
  9.5 0.7 pad_maximum_fusion.refs_3_
  10.2 1.2 fusion.2
  11.4 0.7 dynamic-slice_bitcast_fusion
  12.2 0.3 multiply_cosine_fusion
  12.6 0.7 maximum_maximum_fusion.refs_5_
  13.3 1.0 convert_element_type.21.refs_7_.refs_6_
  14.2 0.7 slice_bitcast_fusion
  15.0 0.8 scatter.19.refs_6_
  15.9 0.6 copy-done.7
  16.4 135.8 %shard_map.203 = (bf16[4,4,2,48,768]{4,3,2,1,0:T(8,128)(2,1)}, bf16[4,4,2,48,1536]{4,3,2,1,0:T(8,128)(2,1)}, bf16[4,4,2,32,1536]{4,3,2,1,0:T(8,128)(2,1)}, bf16[...) custom-call(bf16[48,768]{1,0:T(8,128)(2,1)} %bitcast.95, ...), custom_call_target="tpu_custom_call" | custom-call | tf_op jit(solution)/shard_map/pallas_call | solution.py:103
  152.2 93.0 %shard_map.204 = (bf16[4,4,2,48,1536]{4,3,2,1,0:T(8,128)(2,1)}, bf16[4,4,2,32,1536]{4,3,2,1,0:T(8,128)(2,1)}, bf16[4,4,2,48,2048]{4,3,2,1,0:T(8,128)(2,1)}, bf16...) custom-call(bf16[4,4,2,48,1536]{4,3,2,1,0:T(8,128)(2,1)} %get-tuple-, ...), custom_call_target="tpu_custom_call", output_to_operand_aliasing={{0}: (0, {}), {1}: (1, {}), {2}: (2, {})} | custom-call | tf_op jit(solution)/shard_map/pallas_call | solution.py:103
  245.3 1.0 bitcast_convert_fusion.refs_1_
  246.2 37.8 %shard_map.205 = (bf16[16,32,1536]{2,1,0:T(8,128)(2,1)}, bf16[16,32,1536]{2,1,0:T(8,128)(2,1)}, bf16[16,48,2048]{2,1,0:T(8,128)(2,1)}, bf16[16,48,2048]{2,1,0:T(...) custom-call(bf16[512,1536]{1,0:T(8,128)(2,1)} %bitcast.80, ...), custom_call_target="tpu_custom_call" | custom-call | tf_op jit(solution)/shard_map/pallas_call | solution.py:103
  284.0 64.1 %shard_map.206 = (bf16[16,48,768]{2,1,0:T(8,128)(2,1)}, bf16[16,48,768]{2,1,0:T(8,128)(2,1)}, f32[2,64,1536]{2,1,0:T(8,128)}, bf16[2,64,1536]{2,1,0:T(8,128)(2,1...) custom-call(bf16[8,128,192]{2,1,0:T(8,128)(2,1)} %get-tuple-element.150.refs_0_, ...), custom_call_target="tpu_custom_call" | custom-call | tf_op jit(solution)/shard_map/pallas_call | solution.py:103
  348.1 59.2 %shard_map.207 = (bf16[16,32,1536]{2,1,0:T(8,128)(2,1)}, bf16[16,32,1536]{2,1,0:T(8,128)(2,1)}, bf16[16,48,2048]{2,1,0:T(8,128)(2,1)}, bf16[16,48,2048]{2,1,0:T(...) custom-call(bf16[2,64,1536]{2,1,0:T(8,128)(2,1)} %get-tuple-element., ...), custom_call_target="tpu_custom_call" | custom-call | tf_op jit(solution)/shard_map/pallas_call | solution.py:103
  407.3 102.8 %shard_map.208 = (bf16[16,48,768]{2,1,0:T(8,128)(2,1)}, bf16[16,48,768]{2,1,0:T(8,128)(2,1)}, f32[2,64,1536]{2,1,0:T(8,128)}, bf16[2,64,1536]{2,1,0:T(8,128)(2,1...) custom-call(bf16[8,128,192]{2,1,0:T(8,128)(2,1)} %get-tuple-element., ...), custom_call_target="tpu_custom_call" | custom-call | tf_op jit(solution)/shard_map/pallas_call | solution.py:103
  510.2 1.3 select_maximum_fusion.refs_5_
  511.6 50.0 %shard_map.209 = (bf16[4,48,768]{2,1,0:T(8,128)(2,1)}, bf16[1,48,768]{2,1,0:T(8,128)(2,1)}, bf16[4,48,768]{2,1,0:T(8,128)(2,1)}, bf16[1,48,2048]{2,1,0:T(8,128)(...) custom-call(bf16[4,4,48,768]{3,2,1,0:T(8,128)(2,1)} %bitcast.85, ...), custom_call_target="tpu_custom_call" | custom-call | tf_op jit(solution)/shard_map/pallas_call | solution.py:103
  561.6 8.0 %shard_map.210 = (f32[2,48,1536]{2,1,0:T(8,128)}, f32[2,48,768]{2,1,0:T(8,128)}, f32[2,48,768]{2,1,0:T(8,128)}, f32[2,48,1536]{2,1,0:T(8,128)}, f32[2,48,4096]{2...) custom-call(bf16[4,48,768]{2,1,0:T(8,128)(2,1)} %get-tuple-element.202.refs_0_, ...), custom_call_target="tpu_custom_call" | custom-call | flops 1000000000 | bytes 10000000 | tf_op jit(solution)/shard_map/pallas_call | solution.py:1259
  569.7 0.6 constant_dynamic-slice_fusion.1
  570.3 0.7 copy.69
  571.0 0.9 copy.70
  (57 shorter events, 2.1 us)
Async XLA Ops:
  0.6 5.4 copy-start.2
  3.0 3.6 copy-start.3
  9.1 2.9 copy-start.12
  9.1 4.1 copy-start
  9.2 5.0 copy-start.6
  9.3 5.6 copy-start.13
  9.4 5.6 copy-start.14
  15.8 0.6 copy-start.7
  152.2 93.1 %copy-start.1 = (bf16[2,64,1536]{2,1,0:T(8,128)(2,1)S(1)}, bf16[2,64,1536]{2,1,0:T(8,128)(2,1)}, u32[]{:S(2)}) copy-start(bf16[2,64,1536]{2,1,0:T(8,128)(2,1)} %refs_8_.1) | copy-start | bytes 1179652
  407.3 102.9 %copy-start.9 = (f32[1,1536]{1,0:T(1,128)S(1)}, f32[1,1536]{1,0:T(1,128)}, u32[]{:S(2)}) copy-start(f32[1,1536]{1,0:T(1,128)} %get-tuple-element.200) | copy-start | bytes 18436
  407.3 102.9 %copy-start.10 = (f32[1,1536]{1,0:T(1,128)S(1)}, f32[1,1536]{1,0:T(1,128)}, u32[]{:S(2)}) copy-start(f32[1,1536]{1,0:T(1,128)} %get-tuple-element.198) | copy-start | bytes 18436
  407.3 102.9 %copy-start.11 = (f32[1,1536]{1,0:T(1,128)S(1)}, f32[1,1536]{1,0:T(1,128)}, u32[]{:S(2)}) copy-start(f32[1,1536]{1,0:T(1,128)} %get-tuple-element.199) | copy-start | bytes 18436
  561.6 8.0 %copy-start.8 = (f32[8,1536]{1,0:T(8,128)S(1)}, f32[8,1536]{1,0:T(8,128)}, u32[]{:S(2)}) copy-start(f32[8,1536]{1,0:T(8,128)} %get-tuple-element.201) | copy-start | bytes 147460
  561.6 8.7 %copy-start.5 = (bf16[2,64,1536]{2,1,0:T(8,128)(2,1)S(1)}, bf16[2,64,1536]{2,1,0:T(8,128)(2,1)}, u32[]{:S(2)}) copy-start(bf16[2,64,1536]{2,1,0:T(8,128)(2,1)} %get-tuple-element.258) | copy-start | bytes 1179652
  561.6 9.4 %copy-start.4 = (f32[2,64,1536]{2,1,0:T(8,128)S(1)}, f32[2,64,1536]{2,1,0:T(8,128)}, u32[]{:S(2)}) copy-start(f32[2,64,1536]{2,1,0:T(8,128)} %get-tuple-element.259) | copy-start | bytes 2359300
